TPU v7x, 256 devices: a whole 4x4x8 slice. The times are simulated.
256 devices in a mesh: section: 8 (over x, y_lo), fsdp: 32 (over z, y_hi, core).
Axes of the slice: x: 4, y: 4 (y_hi: 2, y_lo: 2; y = y_hi * 2 + y_lo), z: 8, core: 2. Of those that a mesh axis runs over, the one named last changes fastest.
Arguments:
- upstream: bfloat16 [2, 4096, 4096], P(None, 'fsdp'), may hold values from -6 to 6
- saved_inputs: bfloat16 [8, 2, 2, 4096, 4096], P('section', None, None, 'fsdp'), may hold values from -6 to 6
- queries: bfloat16 [8, 2, 2, 4096, 512], P('section', None, None, 'fsdp'), may hold values from -24 to 24
- keys: bfloat16 [8, 2, 2, 4096, 512], P('section', None, None, 'fsdp'), may hold values from -24 to 24
- segments: int32 [2, 32, 128], P(None, 'fsdp'), may hold values from 0 to 3, never falling along the last dimension, each value on 1 to 64 neighbouring positions
- weights: bfloat16 [8, 2, 4096, 512], P('section', None, 'fsdp'), may hold values from -0.09375 to 0.09375
- gains: float32 [8, 2, 4096], P('section'), may hold values from 0.1 to 1.9
Outputs:
- boundary_grads: bfloat16 [8, 2, 4096, 4096], P('section', None, 'fsdp')
- weight_grad: float32 [8, 2, 4096, 512], P('section', None, 'fsdp')
All inputs are finite; a program needn't handle non-finite values.
Results may differ from a plain program's by a relative error of at most 0.033.
Values may be sent and summed in bfloat16 or wider, within the bound.
No kernel may reach another device: no remote copies, remote signals or barrier semaphores. Data moves between devices by JAX's collectives and lax.ppermute only.
A program may use at most 128 MiB of HBM per device.

v0:
```python
import math

import jax
import jax.numpy as jnp
from jax import lax
from jax.sharding import PartitionSpec as P

HEADS = 4
HEAD_DIM = 128


EPS = 1e-05


def from_behind(value, axis, steps):
    count = lax.axis_size(axis)
    initial, last = (max(0, -steps), min(count, count - steps))
    return lax.ppermute(value, axis, [(source, source + steps) for source in range(initial, last)])


def attention_weights(queries, keys, segment):
    length = queries.shape[0]
    q_heads = queries.reshape(length, HEADS, HEAD_DIM)
    k_heads = keys.reshape(length, HEADS, HEAD_DIM)
    scores = jnp.einsum("tad,sad->ats", q_heads, k_heads, preferred_element_type=jnp.float32) * (
        1.0 / math.sqrt(HEAD_DIM)
    )
    position = jnp.arange(length)
    allowed = (position[:, None] >= position[None, :]) & (segment[:, None] == segment[None, :])
    scores = jnp.where(allowed[None], scores, -1e30)
    peak = jnp.max(scores, -1, keepdims=True)
    expo = jnp.where(allowed[None], jnp.exp(scores - peak), 0.0)
    return (expo / jnp.sum(expo, -1, keepdims=True)).astype(jnp.bfloat16)


def layer_backward(upstream_gradient, xin, queries, keys, segment, weight, norm_gain_vector):
    length = upstream_gradient.shape[0]
    rank = weight.shape[1]
    gathered_input = xin.astype(jnp.float32)
    inverse_norm_scale = lax.rsqrt(
        jnp.mean(gathered_input * gathered_input, -1, keepdims=True) + EPS
    )
    standardized_input = gathered_input * inverse_norm_scale
    normalized_rows = (standardized_input * norm_gain_vector).astype(jnp.bfloat16)
    probs = attention_weights(queries, keys, segment)
    values = jnp.dot(normalized_rows, weight, preferred_element_type=jnp.float32).astype(
        jnp.bfloat16
    )
    value_heads = values.reshape(length, HEADS, HEAD_DIM)
    mixed = (
        jnp.einsum("ats,sad->tad", probs, value_heads, preferred_element_type=jnp.float32)
        .reshape(length, rank)
        .astype(jnp.bfloat16)
    )
    dmix = jnp.dot(upstream_gradient, weight, preferred_element_type=jnp.float32).astype(
        jnp.bfloat16
    )
    dmix_heads = dmix.reshape(length, HEADS, HEAD_DIM)
    dvalues = (
        jnp.einsum("ats,tad->sad", probs, dmix_heads, preferred_element_type=jnp.float32)
        .reshape(length, rank)
        .astype(jnp.bfloat16)
    )
    dnormed = lax.dot_general(
        dvalues, weight, (((1,), (1,)), ((), ())), preferred_element_type=jnp.float32
    )
    centered_input_gradient = dnormed * norm_gain_vector
    backward_output = upstream_gradient.astype(jnp.float32) + inverse_norm_scale * (
        centered_input_gradient
        - standardized_input
        * jnp.mean(centered_input_gradient * standardized_input, -1, keepdims=True)
    )
    return (backward_output.astype(jnp.bfloat16), normalized_rows, mixed, dvalues)


def body(upstream, saved_inputs, queries, keys, segments, weights, gains):
    sections = lax.axis_size("section")
    section_index = lax.axis_index("section")
    shards = lax.axis_size("fsdp")
    batches, length, width = upstream.shape
    rank = weights.shape[3]
    full_weight = lax.all_gather(weights, "fsdp", axis=2, tiled=True)[0]
    saved = saved_inputs[0]
    query_all = queries[0]
    key_all = keys[0]
    gain_all = gains[0]
    segment_rows = segments[:, 0, :]
    contract = (((0,), (0,)), ((), ()))

    def section_backward(upstream_gradient, micro):
        factors = []
        for group in (1, 0):
            xin = lax.dynamic_index_in_dim(saved[group], micro, 0, keepdims=False)
            q_rows = lax.dynamic_index_in_dim(query_all[group], micro, 0, keepdims=False)
            k_rows = lax.dynamic_index_in_dim(key_all[group], micro, 0, keepdims=False)
            segment = lax.dynamic_index_in_dim(segment_rows, micro, 0, keepdims=False)
            backward_output, normalized_rows, mixed, dvalues = layer_backward(
                upstream_gradient, xin, q_rows, k_rows, segment, full_weight[group], gain_all[group]
            )
            left_rows = jnp.concatenate([upstream_gradient, normalized_rows], 0)
            right_rows = jnp.concatenate([mixed, dvalues], 0)
            factors.append((group, left_rows, right_rows))
            upstream_gradient = backward_output
        return (upstream_gradient, factors)

    state = jnp.zeros((width, 2, rank), jnp.float32)

    def update(state, factors):
        for group, left_rows, right_rows in factors:
            state = state.at[:, group].add(
                lax.dot_general(left_rows, right_rows, contract, preferred_element_type=jnp.float32)
            )
        return state

    def tick(step, carry):
        incoming, boundary, state = carry
        micro = step - (sections - 1 - section_index)
        active = (micro >= 0) & (micro < batches)
        micro = jnp.clip(micro, 0, batches - 1)
        top = lax.dynamic_index_in_dim(upstream, micro, 0, keepdims=False)
        upstream_gradient = jnp.where(section_index == sections - 1, top, incoming)

        def working(operands):
            grad_in, boundary_in, state_in = operands
            backward_output, factors = section_backward(grad_in, micro)
            boundary_out = lax.dynamic_update_index_in_dim(boundary_in, backward_output, micro, 0)
            return (backward_output, boundary_out, update(state_in, factors))

        def waiting(operands):
            grad_in, boundary_in, state_in = operands
            return (jnp.zeros_like(grad_in), boundary_in, state_in)

        backward_output, boundary, state = lax.cond(
            active, working, waiting, (upstream_gradient, boundary, state)
        )
        incoming = from_behind(backward_output, "section", -1)
        return (incoming, boundary, state)

    start = (
        jnp.zeros((length, width), jnp.bfloat16),
        jnp.zeros((batches, length, width), jnp.bfloat16),
        state,
    )
    incoming, boundary, state = lax.fori_loop(0, sections + batches - 1, tick, start)
    summed = lax.psum_scatter(
        state.astype(jnp.bfloat16), "fsdp", scatter_dimension=0, tiled=True
    ).astype(jnp.float32)
    weight_grad = jnp.transpose(summed / shards, (1, 0, 2))[None]
    return (boundary[None], weight_grad)


def solution(mesh):
    return jax.shard_map(
        body,
        mesh=mesh,
        in_specs=(
            P(None, "fsdp", None),
            P("section", None, None, "fsdp", None),
            P("section", None, None, "fsdp", None),
            P("section", None, None, "fsdp", None),
            P(None, "fsdp", None),
            P("section", None, "fsdp", None),
            P("section", None, None),
        ),
        out_specs=(P("section", None, "fsdp", None), P("section", None, "fsdp", None)),
        check_vma=False,
    )
```

profile of v0, /device:TPU:1, one launch (start us, length us, event | category | flops | bytes accessed | tf_op | source)
XLA Modules:
  0.0 1087.5 jit_solution(13089994944433340848)
XLA Ops:
  8.0 2.0 copy.29
  10.0 2.1 copy.30
  12.1 104.4 %all-gather.2.cloned.1.call-done = bf16[1,2,4096,512]{3,2,1,0:T(8,128)(2,1)} async-done(((bf16[1,2,128,512]{3,2,1,0:T(8,128)(2,1)}), bf16[1,2,4096,512]{3,2,1,0:T(8,128)(2,1)}) %all-gather.2.cloned.1.call-update) | async-done | bytes 8388624 | tf_op jit(solution)/shard_map/all_gather | solution.py:82
  116.6 1.6 broadcast_in_dim.71
  118.2 7.9 broadcast_in_dim.72
  126.0 793.2 %while.21 = (s32[]{:T(128)}, bf16[128,4096]{1,0:T(8,128)(2,1)S(1)}, bf16[2,128,4096]{2,1,0:T(8,128)(2,1)}, f32[4096,2,512]{2,0,1:T(8,128)}, s32[]{:T(128)}, /*in...) while((s32[]{:T(128)}, bf16[128,4096]{1,0:T(8,128)(2,1)S(1)}, ...), condition=%wide.region_11.12_spmd, body=%wide.region_0.11_spmd.sunk | while | flops 5508876800 | bytes 159062384 | solution.py:144
  127.2 1.3 collective-permute-start
  128.5 25.3 %collective-permute-done = bf16[128,4096]{1,0:T(8,128)(2,1)S(1)} collective-permute-done((bf16[128,4096]{1,0:T(8,128)(2,1)}, bf16[128,4096]{1,0:T(8,128)(2,1)S(1)}, u32[]{:S(2)}, u32[]{:S(2)}) %collective-permute-start) | collective-permute-done | bytes 1048608 | tf_op jit(solution)/shard_map/while/body/eval_jaxpr/ppermute | solution.py:18
  155.0 1.3 collective-permute-start
  156.3 24.4 %collective-permute-done = bf16[128,4096]{1,0:T(8,128)(2,1)S(1)} collective-permute-done((bf16[128,4096]{1,0:T(8,128)(2,1)}, bf16[128,4096]{1,0:T(8,128)(2,1)S(1)}, u32[]{:S(2)}, u32[]{:S(2)}) %collective-permute-start) | collective-permute-done | bytes 1048608 | tf_op jit(solution)/shard_map/while/body/eval_jaxpr/ppermute | solution.py:18
  181.8 1.3 collective-permute-start
  183.1 24.4 %collective-permute-done = bf16[128,4096]{1,0:T(8,128)(2,1)S(1)} collective-permute-done((bf16[128,4096]{1,0:T(8,128)(2,1)}, bf16[128,4096]{1,0:T(8,128)(2,1)S(1)}, u32[]{:S(2)}, u32[]{:S(2)}) %collective-permute-start) | collective-permute-done | bytes 1048608 | tf_op jit(solution)/shard_map/while/body/eval_jaxpr/ppermute | solution.py:18
  208.7 1.3 collective-permute-start
  210.0 23.4 %collective-permute-done = bf16[128,4096]{1,0:T(8,128)(2,1)S(1)} collective-permute-done((bf16[128,4096]{1,0:T(8,128)(2,1)}, bf16[128,4096]{1,0:T(8,128)(2,1)S(1)}, u32[]{:S(2)}, u32[]{:S(2)}) %collective-permute-start) | collective-permute-done | bytes 1048608 | tf_op jit(solution)/shard_map/while/body/eval_jaxpr/ppermute | solution.py:18
  234.6 1.3 collective-permute-start
  235.9 22.5 %collective-permute-done = bf16[128,4096]{1,0:T(8,128)(2,1)S(1)} collective-permute-done((bf16[128,4096]{1,0:T(8,128)(2,1)}, bf16[128,4096]{1,0:T(8,128)(2,1)S(1)}, u32[]{:S(2)}, u32[]{:S(2)}) %collective-permute-start) | collective-permute-done | bytes 1048608 | tf_op jit(solution)/shard_map/while/body/eval_jaxpr/ppermute | solution.py:18
  259.6 1.3 collective-permute-start
  260.9 21.6 %collective-permute-done = bf16[128,4096]{1,0:T(8,128)(2,1)S(1)} collective-permute-done((bf16[128,4096]{1,0:T(8,128)(2,1)}, bf16[128,4096]{1,0:T(8,128)(2,1)S(1)}, u32[]{:S(2)}, u32[]{:S(2)}) %collective-permute-start) | collective-permute-done | bytes 1048608 | tf_op jit(solution)/shard_map/while/body/eval_jaxpr/ppermute | solution.py:18
  284.9 461.8 %collective-permute-done = bf16[128,4096]{1,0:T(8,128)(2,1)S(1)} collective-permute-done((bf16[128,4096]{1,0:T(8,128)(2,1)}, bf16[128,4096]{1,0:T(8,128)(2,1)S(1)}, u32[]{:S(2)}, u32[]{:S(2)}) %collective-permute-start) | collective-permute-done | bytes 1048608 | tf_op jit(solution)/shard_map/while/body/eval_jaxpr/ppermute | solution.py:18
  746.7 64.2 %conditional.2 = (bf16[128,4096]{1,0:T(8,128)(2,1)}, bf16[2,128,4096]{2,1,0:T(8,128)(2,1)}, f32[4096,2,512]{2,0,1:T(8,128)}) conditional(s32[]{:T(128)} %convert_element_type.270, (bf16[2,128,4096]{2,1,0:T(8,128)(2,1)}, f32[4096,2,512]{2,0,1:T(8,128)}) %tuple.74, (pred[]{:T(512)}, s32[]{:T(128)}, bf16[2,128,4096]{2,1,0:T(8,128)(2,1)}, ...), branch_computations={%region_1.1_spmd, %region_2.10_spmd} | conditional | flops 5508876800 | bytes 154867744 | solution.py:133
  747.5 1.5 fusion.100
  749.0 1.3 bitcast_select_fusion
  750.3 2.9 fusion.62
  756.3 2.6 fusion.97
  760.9 3.6 fusion.71
  764.5 1.7 copy.42
  766.2 1.8 convolution_convert_fusion
  768.0 3.6 fusion.65
  771.6 1.7 copy.41
  773.2 2.0 convolution_convert_fusion.1
  775.2 3.8 fusion.30
  779.1 2.0 fusion.35
  781.0 3.6 fusion.68
  784.6 1.7 copy.40
  786.3 1.8 convolution_convert_fusion.2
  788.1 4.3 fusion.44
  792.5 1.7 bitcast_dynamic-update-slice_fusion
  794.2 8.7 fusion.3
  802.9 8.0 fusion.2
  812.2 21.5 %collective-permute-done = bf16[128,4096]{1,0:T(8,128)(2,1)S(1)} collective-permute-done((bf16[128,4096]{1,0:T(8,128)(2,1)}, bf16[128,4096]{1,0:T(8,128)(2,1)S(1)}, u32[]{:S(2)}, u32[]{:S(2)}) %collective-permute-start) | collective-permute-done | bytes 1048608 | tf_op jit(solution)/shard_map/while/body/eval_jaxpr/ppermute | solution.py:18
  833.7 64.2 %conditional.2 = (bf16[128,4096]{1,0:T(8,128)(2,1)}, bf16[2,128,4096]{2,1,0:T(8,128)(2,1)}, f32[4096,2,512]{2,0,1:T(8,128)}) conditional(s32[]{:T(128)} %convert_element_type.270, (bf16[2,128,4096]{2,1,0:T(8,128)(2,1)}, f32[4096,2,512]{2,0,1:T(8,128)}) %tuple.74, (pred[]{:T(512)}, s32[]{:T(128)}, bf16[2,128,4096]{2,1,0:T(8,128)(2,1)}, ...), branch_computations={%region_1.1_spmd, %region_2.10_spmd} | conditional | flops 5508876800 | bytes 154867744 | solution.py:133
  834.5 1.5 fusion.100
  836.0 1.3 bitcast_select_fusion
  837.3 2.9 fusion.62
  843.3 2.6 fusion.97
  847.9 3.7 fusion.71
  851.5 1.7 copy.42
  853.2 1.8 convolution_convert_fusion
  855.0 3.6 fusion.65
  858.6 1.7 copy.41
  860.3 2.0 convolution_convert_fusion.1
  862.3 3.8 fusion.30
  866.1 2.0 fusion.35
  868.1 3.6 fusion.68
  871.6 1.7 copy.40
  873.3 1.8 convolution_convert_fusion.2
  875.1 4.3 fusion.44
  879.5 1.7 bitcast_dynamic-update-slice_fusion
  881.3 8.7 fusion.3
  890.0 8.0 fusion.2
  899.2 20.0 %collective-permute-done = bf16[128,4096]{1,0:T(8,128)(2,1)S(1)} collective-permute-done((bf16[128,4096]{1,0:T(8,128)(2,1)}, bf16[128,4096]{1,0:T(8,128)(2,1)S(1)}, u32[]{:S(2)}, u32[]{:S(2)}) %collective-permute-start) | collective-permute-done | bytes 1048608 | tf_op jit(solution)/shard_map/while/body/eval_jaxpr/ppermute | solution.py:18
  919.2 9.0 convert_element_type.167
  928.3 150.6 %reduce-scatter.2.cloned.1.call-done = bf16[128,2,512]{2,0,1:T(8,128)(2,1)} async-done(((bf16[4096,2,512]{2,0,1:T(8,128)(2,1)}), bf16[128,2,512]{2,0,1:T(8,128)(2,1)}) %reduce-scatter.2.cloned.1.call-update) | async-done | bytes 262160 | tf_op jit(solution)/shard_map/reduce_scatter | solution.py:145
  1078.8 1.8 multiply_bitcast_fusion
  (118 shorter events, 32.6 us)
Async XLA Ops:
  7.2 109.3 %all-gather.2.cloned.1.call-start = ((), (), s32[]{:S(2)}) async-start(), calls=%async_computation.1 | async-start | bytes 8650752 | tf_op jit(solution)/shard_map/all_gather | solution.py:82
  7.9 1071.0 %reduce-scatter.2.cloned.1.call-start = ((), (), s32[]{:S(2)}) async-start(), calls=%async_computation.2 | async-start | bytes 8650752 | tf_op jit(solution)/shard_map/reduce_scatter | solution.py:145
  127.2 26.6 %collective-permute-start = (bf16[128,4096]{1,0:T(8,128)(2,1)}, bf16[128,4096]{1,0:T(8,128)(2,1)S(1)}, u32[]{:S(2)}, u32[]{:S(2)}) collective-permute-start(bf16[128,4096]{1,0:T(8,128)(2,1)} %get-tuple-element.552), channel_id=1, source_target_pairs={{32,0},{64,32},{96,64},{128,96},{160,128},{192,160},{224,192},{33,... | collective-permute-start | bytes 3145736 | tf_op jit(solution)/shard_map/while/body/eval_jaxpr/ppermute | solution.py:18
  155.0 25.7 %collective-permute-start = (bf16[128,4096]{1,0:T(8,128)(2,1)}, bf16[128,4096]{1,0:T(8,128)(2,1)S(1)}, u32[]{:S(2)}, u32[]{:S(2)}) collective-permute-start(bf16[128,4096]{1,0:T(8,128)(2,1)} %get-tuple-element.552), channel_id=1, source_target_pairs={{32,0},{64,32},{96,64},{128,96},{160,128},{192,160},{224,192},{33,... | collective-permute-start | bytes 3145736 | tf_op jit(solution)/shard_map/while/body/eval_jaxpr/ppermute | solution.py:18
  181.8 25.7 %collective-permute-start = (bf16[128,4096]{1,0:T(8,128)(2,1)}, bf16[128,4096]{1,0:T(8,128)(2,1)S(1)}, u32[]{:S(2)}, u32[]{:S(2)}) collective-permute-start(bf16[128,4096]{1,0:T(8,128)(2,1)} %get-tuple-element.552), channel_id=1, source_target_pairs={{32,0},{64,32},{96,64},{128,96},{160,128},{192,160},{224,192},{33,... | collective-permute-start | bytes 3145736 | tf_op jit(solution)/shard_map/while/body/eval_jaxpr/ppermute | solution.py:18
  208.7 24.7 %collective-permute-start = (bf16[128,4096]{1,0:T(8,128)(2,1)}, bf16[128,4096]{1,0:T(8,128)(2,1)S(1)}, u32[]{:S(2)}, u32[]{:S(2)}) collective-permute-start(bf16[128,4096]{1,0:T(8,128)(2,1)} %get-tuple-element.552), channel_id=1, source_target_pairs={{32,0},{64,32},{96,64},{128,96},{160,128},{192,160},{224,192},{33,... | collective-permute-start | bytes 3145736 | tf_op jit(solution)/shard_map/while/body/eval_jaxpr/ppermute | solution.py:18
  234.6 23.8 %collective-permute-start = (bf16[128,4096]{1,0:T(8,128)(2,1)}, bf16[128,4096]{1,0:T(8,128)(2,1)S(1)}, u32[]{:S(2)}, u32[]{:S(2)}) collective-permute-start(bf16[128,4096]{1,0:T(8,128)(2,1)} %get-tuple-element.552), channel_id=1, source_target_pairs={{32,0},{64,32},{96,64},{128,96},{160,128},{192,160},{224,192},{33,... | collective-permute-start | bytes 3145736 | tf_op jit(solution)/shard_map/while/body/eval_jaxpr/ppermute | solution.py:18
  259.6 22.9 %collective-permute-start = (bf16[128,4096]{1,0:T(8,128)(2,1)}, bf16[128,4096]{1,0:T(8,128)(2,1)S(1)}, u32[]{:S(2)}, u32[]{:S(2)}) collective-permute-start(bf16[128,4096]{1,0:T(8,128)(2,1)} %get-tuple-element.552), channel_id=1, source_target_pairs={{32,0},{64,32},{96,64},{128,96},{160,128},{192,160},{224,192},{33,... | collective-permute-start | bytes 3145736 | tf_op jit(solution)/shard_map/while/body/eval_jaxpr/ppermute | solution.py:18
  283.7 463.1 %collective-permute-start = (bf16[128,4096]{1,0:T(8,128)(2,1)}, bf16[128,4096]{1,0:T(8,128)(2,1)S(1)}, u32[]{:S(2)}, u32[]{:S(2)}) collective-permute-start(bf16[128,4096]{1,0:T(8,128)(2,1)} %get-tuple-element.552), channel_id=1, source_target_pairs={{32,0},{64,32},{96,64},{128,96},{160,128},{192,160},{224,192},{33,... | collective-permute-start | bytes 3145736 | tf_op jit(solution)/shard_map/while/body/eval_jaxpr/ppermute | solution.py:18
  754.9 0.7 copy-start.3
  755.1 0.6 copy-start.14
  758.9 1.4 copy-start
  759.0 16.3 %copy-start.2 = (bf16[1,2,128,4096]{3,2,1,0:T(8,128)(2,1)}, bf16[1,2,128,4096]{3,2,1,0:T(8,128)(2,1)S(1)}, u32[]{:S(2)}) copy-start(bf16[1,2,128,4096]{3,2,1,0:T(8,128)(2,1)S(1)} %get-tuple-element.452) | copy-start | bytes 6291460 | tf_op jit(solution)/shard_map/while/body/eval_jaxpr/cond
  759.0 1.9 copy-start.10
  760.4 0.5 copy-start.11
  775.2 3.8 copy-start.9
  775.2 3.8 copy-start.13
  788.1 4.4 copy-start.1
  788.1 4.4 copy-start.7
  788.1 4.4 copy-start.12
  792.5 1.8 copy-start.5
  794.2 8.7 copy-start.8
  794.2 8.7 copy-start.4
  794.2 8.7 copy-start.6
  810.9 22.8 %collective-permute-start = (bf16[128,4096]{1,0:T(8,128)(2,1)}, bf16[128,4096]{1,0:T(8,128)(2,1)S(1)}, u32[]{:S(2)}, u32[]{:S(2)}) collective-permute-start(bf16[128,4096]{1,0:T(8,128)(2,1)} %get-tuple-element.552), channel_id=1, source_target_pairs={{32,0},{64,32},{96,64},{128,96},{160,128},{192,160},{224,192},{33,... | collective-permute-start | bytes 3145736 | tf_op jit(solution)/shard_map/while/body/eval_jaxpr/ppermute | solution.py:18
  841.9 0.7 copy-start.3
  842.1 0.6 copy-start.14
  845.9 1.4 copy-start
  846.0 16.3 %copy-start.2 = (bf16[1,2,128,4096]{3,2,1,0:T(8,128)(2,1)}, bf16[1,2,128,4096]{3,2,1,0:T(8,128)(2,1)S(1)}, u32[]{:S(2)}) copy-start(bf16[1,2,128,4096]{3,2,1,0:T(8,128)(2,1)S(1)} %get-tuple-element.452) | copy-start | bytes 6291460 | tf_op jit(solution)/shard_map/while/body/eval_jaxpr/cond
  846.0 1.9 copy-start.10
  847.4 0.5 copy-start.11
  862.2 3.8 copy-start.9
  862.3 3.8 copy-start.13
  875.1 4.4 copy-start.1
  875.1 4.4 copy-start.7
  875.1 4.4 copy-start.12
  879.5 1.8 copy-start.5
  881.3 8.7 copy-start.8
  881.3 8.7 copy-start.4
  881.3 8.7 copy-start.6
  897.9 21.3 %collective-permute-start = (bf16[128,4096]{1,0:T(8,128)(2,1)}, bf16[128,4096]{1,0:T(8,128)(2,1)S(1)}, u32[]{:S(2)}, u32[]{:S(2)}) collective-permute-start(bf16[128,4096]{1,0:T(8,128)(2,1)} %get-tuple-element.552), channel_id=1, source_target_pairs={{32,0},{64,32},{96,64},{128,96},{160,128},{192,160},{224,192},{33,... | collective-permute-start | bytes 3145736 | tf_op jit(solution)/shard_map/while/body/eval_jaxpr/ppermute | solution.py:18
Sparse Core Ops, SparseCore 0:
  10.8 105.6 all-gather.1
  928.4 150.4 reduce-scatter.1
where the time goes:
time: 1090 us
  waiting for transfers between devices  901 us (83%)
  matrix products  89.7 us (8%)
  local copies, waits for them, and re-layouts  45.4 us (4%)
  other arithmetic  25.4 us (2%)
  between operations  14.1 us (1%)
  starting transfers between devices  11.6 us (1%)
    ppermute x9, waiting for transfers between devices, from_behind(): lax.ppermute(value, axis, [(source, source + steps) for source in range(i...  645 us
    reduce_scatter x1, waiting for transfers between devices, body(): lax.psum_scatter(state.astype(jnp.bfloat16), 'fsdp', scatter_dimension=0,...  151 us
    all_gather x1, waiting for transfers between devices, body(): full_weight = lax.all_gather(weights, 'fsdp', axis=2, tiled=True)[0]  104 us
    dot_general x4, matrix products, update(): lax.dot_general(left_rows, right_rows, contract, preferred_element_type=j...  33.3 us
  transfers between devices with their start and end apart: 11, of which 11 were waited for; matrix products, arithmetic and copies ran while one was open for 0% of the time, Pallas kernels for 0%

commit v1 on v0

v1 whole, which is shorter than its diff:
```python
import functools
import math

import jax
import jax.numpy as jnp
from jax import lax
from jax.experimental import pallas as pl
from jax.experimental.pallas import tpu as pltpu
from jax.sharding import PartitionSpec as P

HEADS = 4
HEAD_DIM = 128
EPS = 1e-05
CHUNK = 512
VMEM_LIMIT = 48 * 1024 * 1024


def pre_kernel(x_ref, q_ref, k_ref, seg_row_ref, seg_col_ref, rstd_ref, probs_ref):
    length, width = x_ref.shape[2:]
    total = jnp.zeros((length, 1), jnp.float32)
    for at in range(0, width, CHUNK):
        part = x_ref[0, 0, :, at : at + CHUNK].astype(jnp.float32)
        total += jnp.sum(part * part, -1, keepdims=True)
    rstd = lax.rsqrt(total / width + EPS)
    rstd_ref[0, 0] = jnp.broadcast_to(rstd, (length, 128))
    rows = lax.broadcasted_iota(jnp.int32, (length, length), 0)
    columns = lax.broadcasted_iota(jnp.int32, (length, length), 1)
    allowed = (rows >= columns) & (seg_col_ref[0] == seg_row_ref[0])
    for head in range(HEADS):
        own = slice(head * HEAD_DIM, (head + 1) * HEAD_DIM)
        scores = lax.dot_general(
            q_ref[0, 0, :, own],
            k_ref[0, 0, :, own],
            (((1,), (1,)), ((), ())),
            preferred_element_type=jnp.float32,
        ) * (1.0 / math.sqrt(HEAD_DIM))
        scores = jnp.where(allowed, scores, -1e30)
        peak = jnp.max(scores, -1, keepdims=True)
        expo = jnp.where(allowed, jnp.exp(scores - peak), 0.0)
        probs = expo / jnp.sum(expo, -1, keepdims=True)
        probs_ref[0, 0, head] = probs.astype(jnp.bfloat16)


def value_kernel(x_ref, rstd_ref, gain_ref, w_ref, probs_ref, vals_ref, mixed_ref):
    batches, length, width = x_ref.shape[1:]
    rank = w_ref.shape[2]
    acc = jnp.zeros((batches * length, rank), jnp.float32)
    for at in range(0, width, CHUNK):
        gain = gain_ref[0, :, at : at + CHUNK]
        normed = [
            (x_ref[0, m, :, at : at + CHUNK].astype(jnp.float32) * rstd_ref[0, m, :, 0:1] * gain)
            .astype(jnp.bfloat16)
            for m in range(batches)
        ]
        acc += jnp.dot(
            jnp.concatenate(normed, 0),
            w_ref[0, at : at + CHUNK, :],
            preferred_element_type=jnp.float32,
        )
    for m in range(batches):
        part = acc[m * length : (m + 1) * length]
        vals_ref[0, m] = part
        values = part.astype(jnp.bfloat16)
        for head in range(HEADS):
            own = slice(head * HEAD_DIM, (head + 1) * HEAD_DIM)
            mixed_ref[0, m, :, own] = jnp.dot(
                probs_ref[0, m, head], values[:, own], preferred_element_type=jnp.float32
            ).astype(jnp.bfloat16)


def tick_kernel(
    place_ref, incoming, upstream, saved, weight, gains, probs, vals, rstd,
    grads_in, dvs_in, boundary_in,
    out, grads, dvs, boundary,
    g_buf, x_buf, w_buf, gain_buf, p_buf, v_buf, r_buf, dv_buf, sems,
):
    del grads_in, dvs_in, boundary_in
    micro, top = place_ref[0], place_ref[1]
    batches = upstream.shape[0]
    width = incoming.shape[1]
    rank = weight.shape[2]
    count = width // CHUNK

    @pl.when((micro >= 0) & (micro < batches))
    def _():
        used = [0]

        def copy(source, target):
            made = pltpu.make_async_copy(source, target, sems.at[used[0]])
            used[0] += 1
            return made

        from_top = copy(upstream.at[micro], g_buf.at[0])
        from_above = pltpu.make_async_copy(incoming, g_buf.at[0], sems.at[used[0] - 1])

        @pl.when(top == 1)
        def _():
            from_top.start()

        @pl.when(top == 0)
        def _():
            from_above.start()

        load_w, load_x, load_p, load_v, load_r = ({}, {}, {}, {}, {})
        load_gain = copy(gains, gain_buf)
        for layer in (1, 0):
            for c in range(count):
                rows = pl.ds(c * CHUNK, CHUNK)
                load_w[layer, c] = copy(weight.at[layer, rows], w_buf.at[layer, rows])
            load_p[layer] = copy(probs.at[layer, micro], p_buf.at[layer])
            load_v[layer] = copy(vals.at[layer, micro], v_buf.at[layer])
            load_r[layer] = copy(rstd.at[layer, micro], r_buf.at[layer])
            load_x[layer] = copy(saved.at[layer, micro], x_buf.at[layer])
        for layer in (1, 0):
            for c in range(count):
                load_w[layer, c].start()
                if layer == 1 and c == 0:
                    load_gain.start()
            load_p[layer].start()
            load_v[layer].start()
            load_r[layer].start()
            load_x[layer].start()

        from_top.wait()
        stores = [copy(g_buf.at[0], grads.at[1, micro])]
        stores[0].start()
        acc = None
        for c in range(count):
            load_w[1, c].wait()
            rows = slice(c * CHUNK, (c + 1) * CHUNK)
            term = jnp.dot(
                g_buf[0, :, rows], w_buf[1, rows, :], preferred_element_type=jnp.float32
            )
            acc = term if acc is None else acc + term
        load_gain.wait()
        for step, layer in enumerate((1, 0)):
            dmix = acc.astype(jnp.bfloat16)
            load_p[layer].wait()
            for head in range(HEADS):
                own = slice(head * HEAD_DIM, (head + 1) * HEAD_DIM)
                dv_buf[layer, :, own] = lax.dot_general(
                    p_buf[layer, head],
                    dmix[:, own],
                    (((0,), (0,)), ((), ())),
                    preferred_element_type=jnp.float32,
                ).astype(jnp.bfloat16)
            stores.append(copy(dv_buf.at[layer], dvs.at[layer, micro]))
            stores[-1].start()
            dv = dv_buf[layer]
            load_v[layer].wait()
            load_r[layer].wait()
            scale = r_buf[layer, :, 0:1]
            mean = jnp.sum(dv.astype(jnp.float32) * v_buf[layer], -1, keepdims=True) / width
            pull = scale * scale * mean
            load_x[layer].wait()
            acc = None
            for c in range(count):
                rows = slice(c * CHUNK, (c + 1) * CHUNK)
                dnormed = lax.dot_general(
                    dv, w_buf[layer, rows, :], (((1,), (1,)), ((), ())),
                    preferred_element_type=jnp.float32,
                )
                lower = (
                    g_buf[step, :, rows].astype(jnp.float32)
                    + scale * (dnormed * gain_buf[layer : layer + 1, rows])
                    - x_buf[layer, :, rows].astype(jnp.float32) * pull
                ).astype(jnp.bfloat16)
                g_buf[step + 1, :, rows] = lower
                if layer == 1:
                    load_w[0, c].wait()
                    term = jnp.dot(
                        lower, w_buf[0, rows, :], preferred_element_type=jnp.float32
                    )
                    acc = term if acc is None else acc + term
            if layer == 1:
                stores.append(copy(g_buf.at[1], grads.at[0, micro]))
                stores[-1].start()
        stores.append(copy(g_buf.at[2], out))
        stores[-1].start()
        stores.append(copy(g_buf.at[2], boundary.at[micro]))
        stores[-1].start()
        for store in stores:
            store.wait()


def weight_kernel(g_ref, x_ref, rstd_ref, gain_ref, mixed_ref, dv_ref, out_ref):
    batches = g_ref.shape[1]
    left, right = ([], [])
    for m in range(batches):
        left.append(g_ref[0, m])
        right.append(mixed_ref[0, m])
    for m in range(batches):
        left.append(
            (x_ref[0, m].astype(jnp.float32) * rstd_ref[0, m, :, 0:1] * gain_ref[0])
            .astype(jnp.bfloat16)
        )
        right.append(dv_ref[0, m])
    out_ref[0] = lax.dot_general(
        jnp.concatenate(left, 0),
        jnp.concatenate(right, 0),
        (((0,), (0,)), ((), ())),
        preferred_element_type=jnp.float32,
    ).astype(jnp.bfloat16)


def params(**more):
    return pltpu.CompilerParams(vmem_limit_bytes=VMEM_LIMIT, **more)


def body(upstream, saved_inputs, queries, keys, segments, weights, gains):
    sections = lax.axis_size("section")
    section_index = lax.axis_index("section")
    shards = lax.axis_size("fsdp")
    batches, length, width = upstream.shape
    rank = weights.shape[3]
    saved = saved_inputs[0]
    seg_row = segments
    seg_col = jnp.transpose(segments, (0, 2, 1))
    gain_rows = gains[0][:, None, :]
    bf16, f32 = (jnp.bfloat16, jnp.float32)
    shape = jax.ShapeDtypeStruct
    any_spec = pl.BlockSpec(memory_space=pl.ANY)

    full_weight = lax.all_gather(weights, "fsdp", axis=2, tiled=True)[0]

    pair = lambda *tail: pl.BlockSpec((1, 1) + tail, lambda l, m: (l, m) + (0,) * len(tail))
    rstd, probs = pl.pallas_call(
        pre_kernel,
        grid=(2, batches),
        in_specs=[
            pair(length, width),
            pair(length, rank),
            pair(length, rank),
            pl.BlockSpec((1, 1, length), lambda l, m: (m, 0, 0)),
            pl.BlockSpec((1, length, 1), lambda l, m: (m, 0, 0)),
        ],
        out_specs=[pair(length, 128), pair(HEADS, length, length)],
        out_shape=[
            shape((2, batches, length, 128), f32),
            shape((2, batches, HEADS, length, length), bf16),
        ],
        compiler_params=params(),
        name="rows_alone",
    )(saved, queries[0], keys[0], seg_row, seg_col)

    each = lambda *tail: pl.BlockSpec((1,) + tail, lambda l: (l,) + (0,) * len(tail))
    vals, mixed = pl.pallas_call(
        value_kernel,
        grid=(2,),
        in_specs=[
            each(batches, length, width),
            each(batches, length, 128),
            each(1, width),
            each(width, rank),
            each(batches, HEADS, length, length),
        ],
        out_specs=[each(batches, length, rank), each(batches, length, rank)],
        out_shape=[
            shape((2, batches, length, rank), f32),
            shape((2, batches, length, rank), bf16),
        ],
        compiler_params=params(),
        name="values",
    )(saved, rstd, gain_rows, full_weight, probs)

    tick = pl.pallas_call(
        tick_kernel,
        in_specs=[pl.BlockSpec(memory_space=pltpu.SMEM)] + [any_spec] * 11,
        out_specs=[any_spec] * 4,
        out_shape=[
            shape((length, width), bf16),
            shape((2, batches, length, width), bf16),
            shape((2, batches, length, rank), bf16),
            shape((batches, length, width), bf16),
        ],
        input_output_aliases={9: 1, 10: 2, 11: 3},
        scratch_shapes=[
            pltpu.VMEM((3, length, width), bf16),
            pltpu.VMEM((2, length, width), bf16),
            pltpu.VMEM((2, width, rank), bf16),
            pltpu.VMEM((2, width), f32),
            pltpu.VMEM((2, HEADS, length, length), bf16),
            pltpu.VMEM((2, length, rank), f32),
            pltpu.VMEM((2, length, 128), f32),
            pltpu.VMEM((2, length, rank), bf16),
            pltpu.SemaphoreType.DMA((40,)),
        ],
        compiler_params=params(),
        name="section",
    )

    incoming = upstream[0]
    grads = jnp.zeros((2, batches, length, width), bf16)
    dvs = jnp.zeros((2, batches, length, rank), bf16)
    boundary = jnp.zeros((batches, length, width), bf16)
    top = (section_index == sections - 1).astype(jnp.int32)
    for step in range(sections + batches - 1):
        micro = step - (sections - 1 - section_index)
        place = jnp.stack([micro.astype(jnp.int32), top])
        out, grads, dvs, boundary = tick(
            place, incoming, upstream, saved, full_weight, gains[0], probs, vals, rstd,
            grads, dvs, boundary,
        )
        if step < sections + batches - 2:
            senders = [sections - 1 - step + m for m in range(batches)]
            incoming = lax.ppermute(
                out, "section", [(s, s - 1) for s in senders if 1 <= s < sections]
            )

    both = lambda *tail: pl.BlockSpec((1, batches) + tail, lambda l, c: (l, 0) + (0,) * len(tail))
    cols = lambda: pl.BlockSpec((1, batches, length, CHUNK), lambda l, c: (l, 0, 0, c))
    partial = pl.pallas_call(
        weight_kernel,
        grid=(2, width // CHUNK),
        in_specs=[
            cols(),
            cols(),
            both(length, 128),
            pl.BlockSpec((1, 1, CHUNK), lambda l, c: (l, 0, c)),
            both(length, rank),
            both(length, rank),
        ],
        out_specs=pl.BlockSpec((1, CHUNK, rank), lambda l, c: (l, c, 0)),
        out_shape=shape((2, width, rank), bf16),
        compiler_params=params(),
        name="partial",
    )(grads, saved, rstd, gain_rows, mixed, dvs)
    summed = lax.psum_scatter(partial, "fsdp", scatter_dimension=1, tiled=True)
    weight_grad = (summed.astype(f32) / shards)[None]
    return (boundary[None], weight_grad)


def solution(mesh):
    return jax.shard_map(
        body,
        mesh=mesh,
        in_specs=(
            P(None, "fsdp", None),
            P("section", None, None, "fsdp", None),
            P("section", None, None, "fsdp", None),
            P("section", None, None, "fsdp", None),
            P(None, "fsdp", None),
            P("section", None, "fsdp", None),
            P("section", None, None),
        ),
        out_specs=(P("section", None, "fsdp", None), P("section", None, "fsdp", None)),
        check_vma=False,
    )
```

time: 1090 us -> 629 us (0.58)
  waiting for transfers between devices: 901 us -> 494 us
  matrix products: 89.7 us -> 0 us
  Pallas kernels: 0 us -> 65.4 us
  other arithmetic: 25.4 us -> 2.5 us
  local copies, waits for them, and re-layouts: 45.4 us -> 33 us
    ppermute x9 -> x8, waiting for transfers between devices: 645 us -> 244 us  [body(): lax.ppermute(out, 'section', [(s, s - 1) for s in senders if 1 <= s < sec...]
    dot_general x28 -> x0, matrix products: 89.7 us -> none  [the longest x4 33.3 us: update(): lax.dot_general(left_rows, right_rows, contract, preferred_element_type=j...]
    pallas_call x0 -> x12, Pallas kernels: none -> 65.4 us  [the longest x9 42.2 us: body(): tick(place, incoming, upstream, saved, full_weight, gains[0], probs, vals...]
    unnamed x2 -> x76, local copies, waits for them, and re-layouts: 4.11 us -> 27.2 us
    convert_element_type x3 -> x0, other arithmetic: 12.9 us -> none  [the longest x1 8.99 us: body(): state.astype(jnp.bfloat16)]
  transfers between devices with their start and end apart: 11 -> 10, of which waited for: 11 -> 4; matrix products, arithmetic and copies ran while one was open for 0% -> 0% of each run, Pallas kernels for 0% -> 0%
where the time goes in v1:
time: 629 us; the launch traced here: 617 us
  waiting for transfers between devices  494 us (79%)
  Pallas kernels  65.4 us (10%)
  local copies, waits for them, and re-layouts  33 us (5%)
  between operations  15 us (2%)
  starting transfers between devices  6.94 us (1%)
    ppermute x8, waiting for transfers between devices, body(): lax.ppermute(out, 'section', [(s, s - 1) for s in senders if 1 <= s < sec...  244 us
    reduce_scatter x1, waiting for transfers between devices, body(): summed = lax.psum_scatter(partial, 'fsdp', scatter_dimension=1, tiled=True)  150 us
    all_gather x1, waiting for transfers between devices, body(): full_weight = lax.all_gather(weights, 'fsdp', axis=2, tiled=True)[0]  99.3 us
    pallas_call x9, Pallas kernels, body(): tick(place, incoming, upstream, saved, full_weight, gains[0], probs, vals...  42.2 us
    unnamed x76, local copies, waits for them, and re-layouts  27.2 us
    pallas_call x1, Pallas kernels, body(): pl.pallas_call(weight_kernel, grid=(2, width // CHUNK), in_specs=[cols(),...  14.6 us
  transfers between devices with their start and end apart: 10, of which 4 were waited for; matrix products, arithmetic and copies ran while one was open for 0% of the time, Pallas kernels for 0%

profile of v1, /device:TPU:1, one launch (start us, length us, event | category | flops | bytes accessed | tf_op | source)
XLA Modules:
  0.0 616.7 jit_solution(12100161000465507569)
XLA Ops:
  7.2 0.7 all-gather.2.cloned.1.call-update
  8.0 0.8 copy.36.seg_col_ref
  8.8 0.8 broadcast_in_dim_squeeze.3.gain_ref
  9.6 2.2 copy-done
  11.8 1.0 copy-done.25
  12.8 1.0 copy-done.26
  13.8 0.7 copy-done.29
  14.5 2.5 rows_alone.1
  17.0 0.1 pad_add_fusion.8.place_ref
  17.1 0.1 slice_bitcast_fusion.incoming
  17.2 99.3 %all-gather.2.cloned.1.call-done = bf16[1,2,4096,512]{3,2,1,0:T(8,128)(2,1)} async-done(((bf16[1,2,128,512]{3,2,1,0:T(8,128)(2,1)}), bf16[1,2,4096,512]{3,2,1,0:T(8,128)(2,1)}) %all-gather.2.cloned.1.call-update) | async-done | bytes 8388624 | tf_op jit(solution)/shard_map/all_gather | solution.py:224
  116.5 6.1 values.1
  122.7 2.6 broadcast_in_dim.15.grads_in
  125.2 1.6 broadcast_in_dim.17.boundary_in
  126.9 0.9 section.9
  127.8 1.0 copy-done.30
  128.8 0.7 collective-permute-start
  129.5 0.1 pad_add_fusion.7.place_ref
  129.6 1.2 copy-done.3
  130.8 1.0 copy-done.10
  131.8 0.9 section.10
  132.8 1.0 copy-done.31
  133.7 0.7 collective-permute-start.1
  134.5 0.1 pad_add_fusion.6.place_ref
  134.5 1.0 copy-done.17
  135.5 1.2 copy-done.18
  136.8 7.6 %section.11 = (bf16[128,4096]{1,0:T(8,128)(2,1)S(1)}, bf16[2,2,128,4096]{3,2,1,0:T(8,128)(2,1)}, bf16[2,2,128,512]{3,2,1,0:T(8,128)(2,1)S(1)}, bf16[2,128,4096]{2,1,0:T(8,128)(2,1)}) custom-call(s32[2]{0:T(128)S(1)} %pad_add_fusion.6.place_ref, bf16[128,4096]{1,0:T(8,128)(2,1)S(1)} %copy-done.18, ...), custom_call_target="tpu_custom_call", output_to_operand_aliasing={{1}: (9, {}), {2}: (10, {}), {3}: (11, {})} | custom-call | tf_op jit(solution)/shard_map/section/pallas_call | solution.py:300
  144.4 1.0 copy-done.32
  145.4 0.7 collective-permute-start.2
  146.1 0.1 pad_add_fusion.5.place_ref
  146.2 1.0 copy-done.19
  147.2 1.0 copy-done.12
  148.2 1.2 copy-done.20
  149.4 0.9 section.12
  150.4 1.0 copy-done.33
  151.3 0.7 collective-permute-start.3
  152.0 0.1 pad_add_fusion.4.place_ref
  152.1 1.0 copy-done.21
  153.1 1.2 copy-done.22
  154.3 0.9 section.13
  155.3 1.0 copy-done.34
  156.2 0.7 collective-permute-start.4
  157.0 0.1 pad_add_fusion.3.place_ref
  157.0 1.0 copy-done.23
  158.0 1.0 copy-done.14
  159.1 1.2 copy-done.24
  160.3 7.3 %section.14 = (bf16[128,4096]{1,0:T(8,128)(2,1)S(1)}, bf16[2,2,128,4096]{3,2,1,0:T(8,128)(2,1)}, bf16[2,2,128,512]{3,2,1,0:T(8,128)(2,1)S(1)}, bf16[2,128,4096]{2,1,0:T(8,128)(2,1)}) custom-call(s32[2]{0:T(128)S(1)} %pad_add_fusion.3.place_ref, bf16[128,4096]{1,0:T(8,128)(2,1)S(1)} %copy-done.24, ...), custom_call_target="tpu_custom_call", output_to_operand_aliasing={{1}: (9, {}), {2}: (10, {}), {3}: (11, {})} | custom-call | tf_op jit(solution)/shard_map/section/pallas_call | solution.py:300
  167.6 1.0 copy-done.35
  168.5 0.7 collective-permute-start.5
  169.3 0.1 pad_add_fusion.2.place_ref
  169.4 0.9 section.15
  170.3 1.0 copy-done.36
  171.3 1.3 collective-permute-start.6
  172.6 0.1 pad_add_fusion.1.place_ref
  172.6 223.4 %collective-permute-done.6.incoming = bf16[128,4096]{1,0:T(8,128)(2,1)S(1)} collective-permute-done((bf16[128,4096]{1,0:T(8,128)(2,1)}, bf16[128,4096]{1,0:T(8,128)(2,1)S(1)}, u32[]{:S(2)}, u32[]{:S(2)}) %collective-permute-start.6) | collective-permute-done | bytes 1048608 | tf_op jit(solution)/shard_map/ppermute | solution.py:306
  396.0 11.1 %section.16 = (bf16[128,4096]{1,0:T(8,128)(2,1)}, bf16[2,2,128,4096]{3,2,1,0:T(8,128)(2,1)}, bf16[2,2,128,512]{3,2,1,0:T(8,128)(2,1)S(1)}, bf16[2,128,4096]{2,1,0:T(8,128)(2,1)}) custom-call(s32[2]{0:T(128)S(1)} %pad_add_fusion.1.place_ref, ...), custom_call_target="tpu_custom_call", output_to_operand_aliasing={{1}: (9, {}), {2}: (10, {}), {3}: (11, {})} | custom-call | tf_op jit(solution)/shard_map/section/pallas_call | solution.py:300
  407.2 1.3 collective-permute-start.7
  408.5 0.1 pad_add_fusion.place_ref
  408.5 20.9 %collective-permute-done.7.incoming = bf16[128,4096]{1,0:T(8,128)(2,1)S(1)} collective-permute-done((bf16[128,4096]{1,0:T(8,128)(2,1)}, bf16[128,4096]{1,0:T(8,128)(2,1)S(1)}, u32[]{:S(2)}, u32[]{:S(2)}) %collective-permute-start.7) | collective-permute-done | bytes 1048608 | tf_op jit(solution)/shard_map/ppermute | solution.py:306
  429.4 11.7 %section.17 = (bf16[128,4096]{1,0:T(8,128)(2,1)}, bf16[2,2,128,4096]{3,2,1,0:T(8,128)(2,1)}, bf16[2,2,128,512]{3,2,1,0:T(8,128)(2,1)S(1)}, bf16[2,128,4096]{2,1,0:T(8,128)(2,1)}) custom-call(s32[2]{0:T(128)S(1)} %pad_add_fusion.place_ref, ...), custom_call_target="tpu_custom_call", output_to_operand_aliasing={{1}: (9, {}), {2}: (10, {}), {3}: (11, {})} | custom-call | tf_op jit(solution)/shard_map/section/pallas_call | solution.py:300
  441.1 2.2 copy-done.1
  443.3 14.6 %partial.1 = bf16[2,4096,512]{2,1,0:T(8,128)(2,1)} custom-call(bf16[2,2,128,4096]{3,2,1,0:T(8,128)(2,1)S(1)} %copy-done.1, bf16[2,2,128,4096]{3,2,1,0:T(8,128)(2,1)} %bitcast.31, f32[2,2,128,128]{3,2,1,0:T(8,128)S(1)} %get-tuple-element.42.rstd_ref.rstd, f32[2,1,4096]{2,1,0:T(1,128)S(1)} %broadcast_in_dim_squeeze.3.gain_ref, ...), custom_call_target="tpu_custom_call" | custom-call | tf_op jit(solution)/shard_map/partial/pallas_call | solution.py:312
  457.9 149.5 %reduce-scatter.2.cloned.1.call-done = bf16[2,128,512]{2,1,0:T(8,128)(2,1)} async-done(((bf16[2,4096,512]{2,1,0:T(8,128)(2,1)}), bf16[2,128,512]{2,1,0:T(8,128)(2,1)}) %reduce-scatter.2.cloned.1.call-update) | async-done | bytes 262160 | tf_op jit(solution)/shard_map/reduce_scatter | solution.py:328
  607.5 1.8 multiply_bitcast_fusion
  (62 shorter events, 0.2 us)
Async XLA Ops:
  7.2 109.3 %all-gather.2.cloned.1.call-start = ((), (), s32[]{:S(2)}) async-start(), calls=%async_computation.1 | async-start | bytes 8650752 | tf_op jit(solution)/shard_map/all_gather | solution.py:224
  7.9 599.6 %reduce-scatter.2.cloned.1.call-start = ((), (), s32[]{:S(2)}) async-start(), calls=%async_computation.2 | async-start | bytes 8650752 | tf_op jit(solution)/shard_map/reduce_scatter | solution.py:328
  9.6 2.2 copy-start
  11.8 1.0 copy-start.25
  12.8 1.0 copy-start.26
  13.8 0.7 copy-start.29
  14.5 2.6 copy-start.37
  17.0 109.8 %copy-start.9 = (bf16[2,2,4,128,128]{4,3,2,1,0:T(8,128)(2,1)}, bf16[2,2,4,128,128]{4,3,2,1,0:T(8,128)(2,1)S(1)}, u32[]{:S(2)}) copy-start(bf16[2,2,4,128,128]{4,3,2,1,0:T(8,128)(2,1)S(1)} %get-tuple-element.41.probs_ref.probs) | copy-start | bytes 1572868
  122.6 2.6 copy-start.27
  122.6 5.1 copy-start.2
  122.6 4.2 copy-start.16
  127.8 1.0 copy-start.30
  128.8 0.8 collective-permute-start
  129.6 1.2 copy-start.3
  130.8 1.0 copy-start.10
  131.8 3.7 copy-start.4
  131.8 3.7 copy-start.11
  132.8 1.0 copy-start.31
  133.7 0.8 collective-permute-start.1
  134.5 1.0 copy-start.17
  135.5 1.2 copy-start.18
  136.8 10.4 %copy-start.5 = (f32[2,2,128,512]{3,2,1,0:T(8,128)S(1)}, f32[2,2,128,512]{3,2,1,0:T(8,128)}, u32[]{:S(2)}) copy-start(f32[2,2,128,512]{3,2,1,0:T(8,128)} %copy-done.2) | copy-start | bytes 3145732
  144.4 1.0 copy-start.32
  145.4 0.8 collective-permute-start.2
  146.2 1.0 copy-start.19
  147.2 1.0 copy-start.12
  148.2 1.2 copy-start.20
  149.4 3.7 copy-start.6
  149.4 3.7 copy-start.13
  150.3 1.0 copy-start.33
  151.3 0.8 collective-permute-start.3
  152.1 1.0 copy-start.21
  153.1 1.2 copy-start.22
  154.3 3.7 copy-start.7
  155.3 1.0 copy-start.34
  156.2 0.8 collective-permute-start.4
  157.0 1.0 copy-start.23
  158.0 1.0 copy-start.14
  159.1 1.2 copy-start.24
  160.3 9.1 %copy-start.8 = (f32[2,2,128,512]{3,2,1,0:T(8,128)S(1)}, f32[2,2,128,512]{3,2,1,0:T(8,128)}, u32[]{:S(2)}) copy-start(f32[2,2,128,512]{3,2,1,0:T(8,128)} %copy-done.2) | copy-start | bytes 3145732
  160.3 9.1 %copy-start.15 = (bf16[2,2,4,128,128]{4,3,2,1,0:T(8,128)(2,1)S(1)}, bf16[2,2,4,128,128]{4,3,2,1,0:T(8,128)(2,1)}, u32[]{:S(2)}) copy-start(bf16[2,2,4,128,128]{4,3,2,1,0:T(8,128)(2,1)} %copy-done.9) | copy-start | bytes 1572868
  167.6 1.0 copy-start.35
  168.5 0.8 collective-permute-start.5
  170.3 1.0 copy-start.36
  171.3 224.8 %collective-permute-start.6 = (bf16[128,4096]{1,0:T(8,128)(2,1)}, bf16[128,4096]{1,0:T(8,128)(2,1)S(1)}, u32[]{:S(2)}, u32[]{:S(2)}) collective-permute-start(bf16[128,4096]{1,0:T(8,128)(2,1)} %copy-done.36), channel_id=1, source_target_pairs={{32,0},{64,32},{33,1},{65,33},{34,2},{66,34},{35,3},{67,35},{36,4}... | collective-permute-start | bytes 3145736 | tf_op jit(solution)/shard_map/ppermute | solution.py:306
  407.2 22.2 %collective-permute-start.7 = (bf16[128,4096]{1,0:T(8,128)(2,1)}, bf16[128,4096]{1,0:T(8,128)(2,1)S(1)}, u32[]{:S(2)}, u32[]{:S(2)}) collective-permute-start(bf16[128,4096]{1,0:T(8,128)(2,1)} %get-tuple-element.72), channel_id=1, source_target_pairs={{32,0},{33,1},{34,2},{35,3},{36,4},{37,5},{38,6},{39,7},{40,8},{41... | collective-permute-start | bytes 3145736 | tf_op jit(solution)/shard_map/ppermute | solution.py:306
  429.4 11.7 %copy-start.28 = (bf16[2,2,128,512]{3,2,1,0:T(8,128)(2,1)S(1)}, bf16[2,2,128,512]{3,2,1,0:T(8,128)(2,1)}, u32[]{:S(2)}) copy-start(bf16[2,2,128,512]{3,2,1,0:T(8,128)(2,1)} %copy-done.27) | copy-start | bytes 1572868
  441.1 2.2 copy-start.1
Sparse Core Ops, SparseCore 0:
  10.8 105.6 all-gather.1
  458.1 149.3 reduce-scatter.1

commit v2 on v1

--- a/solution.py
+++ b/solution.py
@@ -12,7 +12,11 @@
 HEAD_DIM = 128
 EPS = 1e-05
 CHUNK = 512
-VMEM_LIMIT = 48 * 1024 * 1024
+BLOCKS = 16
+RING = 7
+VMEM_LIMIT = 20 * 1024 * 1024
+VMEM_VALUES = 56 * 1024 * 1024
+VMEM_ALL = 62 * 1024 * 1024
 
 
 def pre_kernel(x_ref, q_ref, k_ref, seg_row_ref, seg_col_ref, rstd_ref, probs_ref):
@@ -41,31 +45,61 @@
         probs_ref[0, 0, head] = probs.astype(jnp.bfloat16)
 
 
-def value_kernel(x_ref, rstd_ref, gain_ref, w_ref, probs_ref, vals_ref, mixed_ref):
-    batches, length, width = x_ref.shape[1:]
-    rank = w_ref.shape[2]
-    acc = jnp.zeros((batches * length, rank), jnp.float32)
-    for at in range(0, width, CHUNK):
-        gain = gain_ref[0, :, at : at + CHUNK]
-        normed = [
-            (x_ref[0, m, :, at : at + CHUNK].astype(jnp.float32) * rstd_ref[0, m, :, 0:1] * gain)
-            .astype(jnp.bfloat16)
-            for m in range(batches)
-        ]
-        acc += jnp.dot(
-            jnp.concatenate(normed, 0),
-            w_ref[0, at : at + CHUNK, :],
-            preferred_element_type=jnp.float32,
-        )
-    for m in range(batches):
-        part = acc[m * length : (m + 1) * length]
-        vals_ref[0, m] = part
-        values = part.astype(jnp.bfloat16)
-        for head in range(HEADS):
-            own = slice(head * HEAD_DIM, (head + 1) * HEAD_DIM)
-            mixed_ref[0, m, :, own] = jnp.dot(
-                probs_ref[0, m, head], values[:, own], preferred_element_type=jnp.float32
-            ).astype(jnp.bfloat16)
+def value_kernel(place_ref, *refs):
+    blocks, refs = refs[:BLOCKS], refs[BLOCKS:]
+    saved, rstd, gains, probs, weight, vals, mixed, _, _, _, _, w_buf, x_buf, sems, x_sem, out_sem = refs
+    batches, length, width = saved.shape[1:]
+    rank = w_buf.shape[2]
+    x_copies = [
+        pltpu.make_async_copy(saved.at[layer], x_buf.at[layer], x_sem.at[layer]) for layer in (0, 1)
+    ]
+    loads = [[], []]
+    rows = blocks[0].shape[2]
+    for layer in (1, 0):
+        for at, block in enumerate(blocks):
+            for slot in (0, 1):
+                start = pl.multiple_of(place_ref[2 * at + slot], rows)
+                made = pltpu.make_async_copy(
+                    block.at[slot, layer],
+                    w_buf.at[layer, pl.ds(start, rows)],
+                    sems.at[layer, 2 * at + slot],
+                )
+                made.start()
+                loads[layer].append(made)
+        x_copies[layer].start()
+    stores = []
+    for layer in (1, 0):
+        for made in loads[layer]:
+            made.wait()
+        store = pltpu.make_async_copy(w_buf.at[layer], weight.at[layer], out_sem.at[layer])
+        store.start()
+        stores.append(store)
+        x_copies[layer].wait()
+        acc = jnp.zeros((batches * length, rank), jnp.float32)
+        for at in range(0, width, CHUNK):
+            cut = slice(at, at + CHUNK)
+            gain = gains[layer : layer + 1, cut]
+            normed = [
+                (x_buf[layer, m, :, cut].astype(jnp.float32) * rstd[layer, m, :, 0:1] * gain)
+                .astype(jnp.bfloat16)
+                for m in range(batches)
+            ]
+            acc += jnp.dot(
+                jnp.concatenate(normed, 0),
+                w_buf[layer, cut, :],
+                preferred_element_type=jnp.float32,
+            )
+        for m in range(batches):
+            part = acc[m * length : (m + 1) * length]
+            vals[layer, m] = part
+            values = part.astype(jnp.bfloat16)
+            for head in range(HEADS):
+                own = slice(head * HEAD_DIM, (head + 1) * HEAD_DIM)
+                mixed[layer, m, :, own] = jnp.dot(
+                    probs[layer, m, head], values[:, own], preferred_element_type=jnp.float32
+                ).astype(jnp.bfloat16)
+    for store in stores:
+        store.wait()
 
 
 def tick_kernel(
@@ -111,19 +145,16 @@
             load_v[layer] = copy(vals.at[layer, micro], v_buf.at[layer])
             load_r[layer] = copy(rstd.at[layer, micro], r_buf.at[layer])
             load_x[layer] = copy(saved.at[layer, micro], x_buf.at[layer])
-        for layer in (1, 0):
-            for c in range(count):
-                load_w[layer, c].start()
-                if layer == 1 and c == 0:
-                    load_gain.start()
-            load_p[layer].start()
-            load_v[layer].start()
-            load_r[layer].start()
-            load_x[layer].start()
+        for c in range(count):
+            load_w[1, c].start()
+        for made in (load_p[1], load_v[1], load_r[1], load_gain, load_x[1]):
+            made.start()
+        for c in range(count):
+            load_w[0, c].start()
+        for made in (load_p[0], load_v[0], load_r[0], load_x[0]):
+            made.start()
 
         from_top.wait()
-        stores = [copy(g_buf.at[0], grads.at[1, micro])]
-        stores[0].start()
         acc = None
         for c in range(count):
             load_w[1, c].wait()
@@ -132,6 +163,8 @@
                 g_buf[0, :, rows], w_buf[1, rows, :], preferred_element_type=jnp.float32
             )
             acc = term if acc is None else acc + term
+        stores = [copy(g_buf.at[0], grads.at[1, micro])]
+        stores[0].start()
         load_gain.wait()
         for step, layer in enumerate((1, 0)):
             dmix = acc.astype(jnp.bfloat16)
@@ -183,28 +216,160 @@
             store.wait()
 
 
-def weight_kernel(g_ref, x_ref, rstd_ref, gain_ref, mixed_ref, dv_ref, out_ref):
-    batches = g_ref.shape[1]
-    left, right = ([], [])
-    for m in range(batches):
-        left.append(g_ref[0, m])
-        right.append(mixed_ref[0, m])
-    for m in range(batches):
-        left.append(
-            (x_ref[0, m].astype(jnp.float32) * rstd_ref[0, m, :, 0:1] * gain_ref[0])
-            .astype(jnp.bfloat16)
-        )
-        right.append(dv_ref[0, m])
-    out_ref[0] = lax.dot_general(
-        jnp.concatenate(left, 0),
-        jnp.concatenate(right, 0),
-        (((0,), (0,)), ((), ())),
-        preferred_element_type=jnp.float32,
-    ).astype(jnp.bfloat16)
-
-
-def params(**more):
-    return pltpu.CompilerParams(vmem_limit_bytes=VMEM_LIMIT, **more)
+def transpose_kernel(mixed_ref, dv_ref, right_ref):
+    batches, length = mixed_ref.shape[1:3]
+    rows = batches * length
+    for layer in (0, 1):
+        for m in range(batches):
+            at = m * length
+            right_ref[layer, :, at : at + length] = mixed_ref[layer, m].T
+            right_ref[layer, :, rows + at : rows + at + length] = dv_ref[layer, m].T
+
+
+def weight_kernel(split, tiles, place_ref, g_ref, x_ref, rstd_ref, gain_ref, right_ref, *refs):
+    first_out, second_out, buf, sems = refs
+    batches, length = g_ref.shape[1:3]
+    wide = 2 * length
+
+    def store(tile, slot, target, at):
+        return pltpu.make_async_copy(buf.at[slot], target.at[at], sems.at[slot])
+
+    def step(tile, carry):
+        slot = lax.rem(tile, 2)
+        start = pl.multiple_of(place_ref[tile] * wide, wide)
+        cut = pl.ds(start, wide)
+
+        @pl.when(tile >= 2)
+        def _():
+            store(tile, slot, first_out, 0).wait()
+
+        for layer in (0, 1):
+            left = [g_ref[layer, m, :, cut] for m in range(batches)]
+            left += [
+                (
+                    x_ref[layer, m, :, cut].astype(jnp.float32)
+                    * rstd_ref[layer, m, :, 0:1]
+                    * gain_ref[layer : layer + 1, cut]
+                ).astype(jnp.bfloat16)
+                for m in range(batches)
+            ]
+            result = jnp.dot(
+                right_ref[layer], jnp.concatenate(left, 0), preferred_element_type=jnp.float32
+            ).astype(jnp.bfloat16)
+            turned = place_ref[tiles + tile]
+            buf[slot, turned, layer] = result[:, :length]
+            buf[slot, 1 - turned, layer] = result[:, length:]
+
+        @pl.when(tile < split)
+        def _():
+            store(tile, slot, first_out, jnp.minimum(tile, split - 1)).start()
+
+        @pl.when(tile >= split)
+        def _():
+            store(tile, slot, second_out, jnp.maximum(tile - split, 0)).start()
+
+        return carry
+
+    lax.fori_loop(0, tiles, step, 0)
+    for tile in (tiles - 2, tiles - 1):
+        store(tile, tile % 2, first_out, 0).wait()
+
+
+def params(limit=VMEM_LIMIT):
+    return pltpu.CompilerParams(vmem_limit_bytes=limit)
+
+
+def other_core(value, shards):
+    return lax.ppermute(value, "fsdp", [(d, d ^ 1) for d in range(shards)])
+
+
+def other_y(value, shards):
+    return lax.ppermute(value, "fsdp", [(d, d ^ 2) for d in range(shards)])
+
+
+def along_z(value, shards):
+    return lax.ppermute(
+        value, "fsdp", [(d, (d + (4 if d % 2 == 0 else shards - 4)) % shards) for d in range(shards)]
+    )
+
+
+def gather_blocks(own_rows, shards, core, early):
+    near = jnp.stack([own_rows, other_core(own_rows, shards)])
+    rows_near = [near]
+    far_rows = other_y(own_rows, shards)
+    near = along_z(near, shards)
+    near, far_rows = lax.optimization_barrier((near, far_rows))
+    rows_near += [near, other_core(near, shards)]
+    far = jnp.stack([far_rows, other_core(far_rows, shards)])
+    rows_far = [far]
+    for k in (1, 2, 3):
+        if k == 2:
+            far, early = lax.optimization_barrier((far, early))
+        if k > 1:
+            near = along_z(near, shards)
+            rows_near += [near, other_core(near, shards)]
+        far = along_z(far, shards)
+        rows_far += [far, other_core(far, shards)]
+    last = along_z(jnp.where(core == 0, near, far), shards)
+    return rows_near + rows_far + [last, other_core(last, shards)], early
+
+
+def in_turn(value, pairs, shards):
+    axes = ("section", "fsdp")
+    half = value.shape[0] // 2
+
+    def of_core(core):
+        return [(a * shards + d, b * shards + d) for a, b in pairs for d in range(core, shards, 2)]
+
+    upper = lax.ppermute(value[:half], axes, of_core(0))
+    lower = lax.ppermute(value[half:], axes, of_core(0))
+    word = lax.ppermute(
+        upper[:8, :128], axes, [(a * shards + d, a * shards + d + 1) for a, _ in pairs for d in range(0, shards, 2)]
+    )
+    word, value = lax.optimization_barrier((word, value))
+    return jnp.concatenate([upper, lower]) + lax.ppermute(value, axes, of_core(1))
+
+
+def add_kernel(*refs):
+    total = refs[0][...].astype(jnp.float32)
+    for ref in refs[1:-1]:
+        total += ref[...].astype(jnp.float32)
+    refs[-1][...] = total.astype(jnp.bfloat16).reshape(refs[-1].shape)
+
+
+def rounded_sum(*terms):
+    block = terms[0][0].shape[1:]
+
+    def spec(at):
+        return pl.BlockSpec((1, 1) + block[1:], lambda i: (at, i) + (0,) * (len(block) - 1))
+
+    return pl.pallas_call(
+        add_kernel,
+        grid=(block[0],),
+        in_specs=[spec(at) for _, at in terms],
+        out_specs=pl.BlockSpec((1,) + block[1:], lambda i: (i,) + (0,) * (len(block) - 1)),
+        out_shape=jax.ShapeDtypeStruct(block, jnp.bfloat16),
+        compiler_params=params(),
+        name="plus",
+    )(*[array for array, _ in terms])
+
+
+def scatter_sum(keep, first, send, own, shards, core):
+    taken_first = other_core(first, shards)
+    taken = other_core(send, shards)
+    came = along_z(rounded_sum((keep, 0), (taken_first, 0)), shards)
+    zero = jnp.zeros_like(came)
+    far = rounded_sum((keep, 2), (taken, 1), (jnp.where(core == 1, came, zero)[None], 0))
+    near = rounded_sum((keep, 1), (taken, 0), (jnp.where(core == 0, came, zero)[None], 0))
+    for k in (1, 2, 3):
+        far = along_z(far, shards)
+        near = along_z(near, shards)
+        far = rounded_sum((far[None], 0), *([(keep, 2 * k + 2), (taken, 2 * k + 1)] if k < 3 else [(own, 1)]))
+        near = rounded_sum((near[None], 0), *([(keep, 2 * k + 1), (taken, 2 * k)] if k < 3 else [(own, 0)]))
+    far_own = far[0].astype(jnp.float32) + other_core(far[1], shards).astype(jnp.float32)
+    far_own = other_y(far_own.astype(jnp.bfloat16), shards).astype(jnp.float32)
+    near_own = near[0].astype(jnp.float32) + other_core(near[1], shards).astype(jnp.float32)
+    return near_own + far_own
 
 
 def body(upstream, saved_inputs, queries, keys, segments, weights, gains):
@@ -216,13 +381,14 @@
     saved = saved_inputs[0]
     seg_row = segments
     seg_col = jnp.transpose(segments, (0, 2, 1))
-    gain_rows = gains[0][:, None, :]
     bf16, f32 = (jnp.bfloat16, jnp.float32)
     shape = jax.ShapeDtypeStruct
     any_spec = pl.BlockSpec(memory_space=pl.ANY)
 
-    full_weight = lax.all_gather(weights, "fsdp", axis=2, tiled=True)[0]
-
+    position = lax.axis_index("fsdp").astype(jnp.int32)
+    z, y_hi, core = position // 4, position // 2 % 2, position % 2
+    chips = shards // 4
+    own_rows = weights[0]
     pair = lambda *tail: pl.BlockSpec((1, 1) + tail, lambda l, m: (l, m) + (0,) * len(tail))
     rstd, probs = pl.pallas_call(
         pre_kernel,
@@ -243,36 +409,58 @@
         name="rows_alone",
     )(saved, queries[0], keys[0], seg_row, seg_col)
 
-    each = lambda *tail: pl.BlockSpec((1,) + tail, lambda l: (l,) + (0,) * len(tail))
-    vals, mixed = pl.pallas_call(
+    gathered, (rstd, probs) = gather_blocks(own_rows, shards, core, (rstd, probs))
+
+    turn = 1 - 2 * core
+    starts = []
+
+    def row_of(chip, high, low):
+        return chip % chips * 4 * length + high * 2 * length + low * length
+
+    for high in (y_hi, 1 - y_hi):
+        starts += [row_of(z, high, core), row_of(z, high, 1 - core)]
+        for k in (1, 2, 3):
+            starts += [row_of(z - turn * k + chips, high, core), row_of(z - turn * k + chips, high, 1 - core)]
+            starts += [row_of(z + turn * k + chips, high, 1 - core), row_of(z + turn * k + chips, high, core)]
+    far = y_hi ^ core
+    starts += [row_of(z + 4, far, core), row_of(z + 4, far, 1 - core)]
+    starts += [row_of(z + 4, 1 - far, 1 - core), row_of(z + 4, 1 - far, core)]
+    smem = pl.BlockSpec(memory_space=pltpu.SMEM)
+    vmem = pl.BlockSpec(memory_space=pltpu.VMEM)
+    hbm = pl.BlockSpec(memory_space=pltpu.HBM)
+    grads_shape = shape((2, batches, length, width), bf16)
+    dvs_shape = shape((2, batches, length, rank), bf16)
+    boundary_shape = shape((batches, length, width), bf16)
+    out_shape = shape((length, width), bf16)
+    full_weight, vals, mixed, grads, dvs, boundary, incoming = pl.pallas_call(
         value_kernel,
-        grid=(2,),
-        in_specs=[
-            each(batches, length, width),
-            each(batches, length, 128),
-            each(1, width),
-            each(width, rank),
-            each(batches, HEADS, length, length),
-        ],
-        out_specs=[each(batches, length, rank), each(batches, length, rank)],
+        in_specs=[smem] + [hbm] * (BLOCKS + 1) + [vmem] * 3,
+        out_specs=[hbm, vmem, vmem] + [hbm] * 4,
         out_shape=[
+            shape((2, width, rank), bf16),
             shape((2, batches, length, rank), f32),
             shape((2, batches, length, rank), bf16),
+            grads_shape,
+            dvs_shape,
+            boundary_shape,
+            out_shape,
         ],
-        compiler_params=params(),
+        scratch_shapes=[
+            pltpu.VMEM((2, width, rank), bf16),
+            pltpu.VMEM((2, batches, length, width), bf16),
+            pltpu.SemaphoreType.DMA((2, 2 * BLOCKS)),
+            pltpu.SemaphoreType.DMA((2,)),
+            pltpu.SemaphoreType.DMA((2,)),
+        ],
+        compiler_params=params(VMEM_VALUES),
         name="values",
-    )(saved, rstd, gain_rows, full_weight, probs)
+    )(jnp.stack(starts), *gathered, saved, rstd, gains[0], probs)
 
     tick = pl.pallas_call(
         tick_kernel,
-        in_specs=[pl.BlockSpec(memory_space=pltpu.SMEM)] + [any_spec] * 11,
-        out_specs=[any_spec] * 4,
-        out_shape=[
-            shape((length, width), bf16),
-            shape((2, batches, length, width), bf16),
-            shape((2, batches, length, rank), bf16),
-            shape((batches, length, width), bf16),
-        ],
+        in_specs=[smem] + [hbm] * 11,
+        out_specs=[hbm] * 4,
+        out_shape=[out_shape, grads_shape, dvs_shape, boundary_shape],
         input_output_aliases={9: 1, 10: 2, 11: 3},
         scratch_shapes=[
             pltpu.VMEM((3, length, width), bf16),
@@ -285,14 +473,10 @@
             pltpu.VMEM((2, length, rank), bf16),
             pltpu.SemaphoreType.DMA((40,)),
         ],
-        compiler_params=params(),
+        compiler_params=params(VMEM_ALL),
         name="section",
     )
 
-    incoming = upstream[0]
-    grads = jnp.zeros((2, batches, length, width), bf16)
-    dvs = jnp.zeros((2, batches, length, rank), bf16)
-    boundary = jnp.zeros((batches, length, width), bf16)
     top = (section_index == sections - 1).astype(jnp.int32)
     for step in range(sections + batches - 1):
         micro = step - (sections - 1 - section_index)
@@ -303,30 +487,45 @@
         )
         if step < sections + batches - 2:
             senders = [sections - 1 - step + m for m in range(batches)]
-            incoming = lax.ppermute(
-                out, "section", [(s, s - 1) for s in senders if 1 <= s < sections]
-            )
-
-    both = lambda *tail: pl.BlockSpec((1, batches) + tail, lambda l, c: (l, 0) + (0,) * len(tail))
-    cols = lambda: pl.BlockSpec((1, batches, length, CHUNK), lambda l, c: (l, 0, 0, c))
-    partial = pl.pallas_call(
-        weight_kernel,
-        grid=(2, width // CHUNK),
-        in_specs=[
-            cols(),
-            cols(),
-            both(length, 128),
-            pl.BlockSpec((1, 1, CHUNK), lambda l, c: (l, 0, c)),
-            both(length, rank),
-            both(length, rank),
-        ],
-        out_specs=pl.BlockSpec((1, CHUNK, rank), lambda l, c: (l, c, 0)),
-        out_shape=shape((2, width, rank), bf16),
+            pairs = [(s, s - 1) for s in senders if 1 <= s < sections]
+            if step == 0:
+                incoming = in_turn(out, pairs, shards)
+            else:
+                incoming = lax.ppermute(out, "section", pairs)
+
+    def tiles_of(low):
+        way = 1 - 2 * low
+        tiles = [(z + 4) % chips * 2 + (y_hi ^ low)]
+        for k in (3, 2, 1):
+            for high in (y_hi, 1 - y_hi):
+                tiles.append((z + way * k + chips) % chips * 2 + high)
+        return tiles
+
+    right = pl.pallas_call(
+        transpose_kernel,
+        in_specs=[vmem] * 2,
+        out_specs=vmem,
+        out_shape=shape((2, rank, 2 * batches * length), bf16),
         compiler_params=params(),
-        name="partial",
-    )(grads, saved, rstd, gain_rows, mixed, dvs)
-    summed = lax.psum_scatter(partial, "fsdp", scatter_dimension=1, tiled=True)
-    weight_grad = (summed.astype(f32) / shards)[None]
+        name="factors",
+    )(mixed, dvs)
+    block = (2, 2, rank, length)
+
+    def partial(tiles, low, split):
+        return pl.pallas_call(
+            functools.partial(weight_kernel, split, len(tiles)),
+            in_specs=[smem] + [vmem] * 5,
+            out_specs=[hbm] * 2,
+            out_shape=[shape((split,) + block, bf16), shape((len(tiles) - split,) + block, bf16)],
+            scratch_shapes=[pltpu.VMEM((2,) + block, bf16), pltpu.SemaphoreType.DMA((2,))],
+            compiler_params=params(),
+            name="partial",
+        )(jnp.stack(tiles + [low] * len(tiles)), grads, saved, rstd, gains[0], right)
+
+    first, send = partial(tiles_of(1 - core), 1 - core, 1)
+    keep, own = partial(tiles_of(core) + [z * 2 + y_hi, z * 2 + 1 - y_hi], core, RING)
+    summed = scatter_sum(keep, first, send, own, shards, core)
+    weight_grad = (jnp.transpose(summed, (0, 2, 1)) / shards)[None]
     return (boundary[None], weight_grad)
 
 

time: 629 us -> 470 us (0.75)
  waiting for transfers between devices: 494 us -> 295 us
  starting transfers between devices: 6.94 us -> 68.7 us
  between operations: 15 us -> 1.7 us
  other arithmetic: 2.5 us -> 9.16 us
    reduce_scatter x1 -> x0, waiting for transfers between devices: 150 us -> none  [body(): summed = lax.psum_scatter(partial, 'fsdp', scatter_dimension=1, tiled=True)]
    all_gather x1 -> x0, waiting for transfers between devices: 99.3 us -> none  [body(): full_weight = lax.all_gather(weights, 'fsdp', axis=2, tiled=True)[0]]
    ppermute x8 -> x39, starting transfers between devices: 6.87 us -> 68.7 us  [the longest x14 29.8 us: along_z(): lax.ppermute(value, 'fsdp', [(d, (d + (4 if d % 2 == 0 else shards - 4))...]
    ppermute x8 -> x39, waiting for transfers between devices: 244 us -> 295 us  [the longest x7 232 us: body(): incoming = lax.ppermute(out, 'section', pairs)]
    pallas_call x9, Pallas kernels: 42.2 us -> 29.6 us  [body(): tick(place, incoming, upstream, saved, full_weight, gains[0], probs, vals...]
    pallas_call x2 -> x13, Pallas kernels: 20.7 us -> 27.5 us  [the longest x1 12.1 us: body(): pl.pallas_call(value_kernel, in_specs=[smem] + [hbm] * (BLOCKS + 1) + [vm...]
    unnamed x76 -> x75, local copies, waits for them, and re-layouts: 27.2 us -> 25.2 us
  transfers between devices with their start and end apart: 10 -> 39, of which waited for: 4 -> 19; matrix products, arithmetic and copies ran while one was open for 0% -> 2% of each run, Pallas kernels for 0% -> 3%
where the time goes in v2:
time: 470 us; the launch traced here: 461 us
  waiting for transfers between devices  295 us (63%)
  starting transfers between devices  68.7 us (15%)
  Pallas kernels  59.6 us (13%)
  local copies, waits for them, and re-layouts  27.4 us (6%)
  other arithmetic  9.16 us (2%)
    ppermute x7, waiting for transfers between devices, body(): incoming = lax.ppermute(out, 'section', pairs)  232 us
    ppermute x14, waiting for transfers between devices, along_z(): lax.ppermute(value, 'fsdp', [(d, (d + (4 if d % 2 == 0 else shards - 4))...  48.6 us
    ppermute x14, starting transfers between devices, along_z(): lax.ppermute(value, 'fsdp', [(d, (d + (4 if d % 2 == 0 else shards - 4))...  29.8 us
    pallas_call x9, Pallas kernels, body(): tick(place, incoming, upstream, saved, full_weight, gains[0], probs, vals...  29.6 us
    unnamed x75, local copies, waits for them, and re-layouts  25.2 us
    ppermute x13, starting transfers between devices, other_core(): return lax.ppermute(value, 'fsdp', [(d, d ^ 1) for d in range(shards)])  24.8 us
    pallas_call x1, Pallas kernels, body(): pl.pallas_call(value_kernel, in_specs=[smem] + [hbm] * (BLOCKS + 1) + [vm...  12.1 us
    pallas_call x2, Pallas kernels, partial(): pl.pallas_call(functools.partial(weight_kernel, split, len(tiles)), in_sp...  11.1 us
  transfers between devices with their start and end apart: 39, of which 19 were waited for; matrix products, arithmetic and copies ran while one was open for 2% of the time, Pallas kernels for 3%

profile of v2, /device:TPU:1, one launch (start us, length us, event | category | flops | bytes accessed | tf_op | source)
XLA Modules:
  0.0 461.4 jit_solution(12509395029539725400)
XLA Ops:
  0.7 3.3 collective-permute-start
  4.0 1.4 collective-permute-done
  5.4 1.0 pad_maximum_fusion.refs_0_
  6.4 3.9 collective-permute-start.1
  10.3 2.9 collective-permute-start.2
  13.2 4.0 collective-permute-done.2
  18.1 1.2 collective-permute-done.8
  19.3 3.4 collective-permute-start.9
  22.9 2.2 copy-done
  25.1 2.5 rows_alone.1
  29.9 2.2 collective-permute-start.11
  32.0 5.4 %collective-permute-done.4.refs_3_ = bf16[2,2,128,512]{3,2,1,0:T(8,128)(2,1)} collective-permute-done((bf16[2,2,128,512]{3,2,1,0:T(8,128)(2,1)S(1)}, bf16[2,2,128,512]{3,2,1,0:T(8,128)(2,1)}, u32[]{:S(2)}, u32[]{:S(2)}) %collective-permute-start.4) | collective-permute-done | bytes 524320 | tf_op jit(solution)/shard_map/ppermute | solution.py:291
  37.4 1.8 collective-permute-start.6
  39.2 3.9 collective-permute-done.11.refs_10_
  43.1 1.6 collective-permute-start.13
  45.2 3.5 collective-permute-done.6.refs_5_
  48.7 5.3 %collective-permute-done.13.refs_12_ = bf16[2,2,128,512]{3,2,1,0:T(8,128)(2,1)S(1)} collective-permute-done((bf16[2,2,128,512]{3,2,1,0:T(8,128)(2,1)S(1)}, bf16[2,2,128,512]{3,2,1,0:T(8,128)(2,1)S(1)}, u32[]{:S(2)}, u32[]{:S(2)}) %collective-permute-start.13) | collective-permute-done | bytes 524320 | tf_op jit(solution)/shard_map/ppermute | solution.py:291
  54.1 2.0 collective-permute-start.15
  57.1 5.5 %collective-permute-done.15.refs_14_ = bf16[2,2,128,512]{3,2,1,0:T(8,128)(2,1)} collective-permute-done((bf16[2,2,128,512]{3,2,1,0:T(8,128)(2,1)S(1)}, bf16[2,2,128,512]{3,2,1,0:T(8,128)(2,1)}, u32[]{:S(2)}, u32[]{:S(2)}) %collective-permute-start.15) | collective-permute-done | bytes 524320 | tf_op jit(solution)/shard_map/ppermute | solution.py:291
  62.6 2.2 collective-permute-start.16
  66.8 12.1 %values.1 = (bf16[2,4096,512]{2,1,0:T(8,128)(2,1)}, f32[2,2,128,512]{3,2,1,0:T(8,128)}, bf16[2,2,128,512]{3,2,1,0:T(8,128)(2,1)}, bf16[2,2,128,4096]{3,2,1,0:T(8...) custom-call(s32[32]{0:T(128)} %stack.308.place_ref, ...), custom_call_target="tpu_custom_call" | custom-call | tf_op jit(solution)/shard_map/values/pallas_call | solution.py:435
  79.0 1.0 section.9
  80.8 1.3 fusion.4
  84.1 1.2 maximum_add_fusion.incoming
  85.3 1.0 section.10
  88.7 1.4 section.11
  92.5 1.0 section.12
  95.8 1.0 section.13
  99.2 1.2 section.14
  102.8 1.0 section.15
  103.8 1.3 collective-permute-start.25
  105.7 214.2 %collective-permute-done.25.incoming = bf16[128,4096]{1,0:T(8,128)(2,1)S(1)} collective-permute-done((bf16[128,4096]{1,0:T(8,128)(2,1)}, bf16[128,4096]{1,0:T(8,128)(2,1)S(1)}, u32[]{:S(2)}, u32[]{:S(2)}) %collective-permute-start.25) | collective-permute-done | bytes 1048608 | tf_op jit(solution)/shard_map/ppermute | solution.py:494
  320.8 10.8 %section.16 = (bf16[128,4096]{1,0:T(8,128)(2,1)}, bf16[2,2,128,4096]{3,2,1,0:T(8,128)(2,1)}, bf16[2,2,128,512]{3,2,1,0:T(8,128)(2,1)}, bf16[2,128,4096]{2,1,0:T(8,128)(2,1)}) custom-call(s32[2]{0:T(128)} %pad_add_fusion.1.place_ref, bf16[128,4096]{1,0:T(8,128)(2,1)} %copy-done.30, ...), custom_call_target="tpu_custom_call", output_to_operand_aliasing={{1}: (9, {}), {2}: (10, {}), {3}: (11, {})} | custom-call | tf_op jit(solution)/shard_map/section/pallas_call | solution.py:484
  331.6 1.3 collective-permute-start.26
  333.7 18.1 %collective-permute-done.26.incoming = bf16[128,4096]{1,0:T(8,128)(2,1)S(1)} collective-permute-done((bf16[128,4096]{1,0:T(8,128)(2,1)}, bf16[128,4096]{1,0:T(8,128)(2,1)S(1)}, u32[]{:S(2)}, u32[]{:S(2)}) %collective-permute-start.26) | collective-permute-done | bytes 1048608 | tf_op jit(solution)/shard_map/ppermute | solution.py:494
  351.8 1.0 copy-done.24
  352.9 11.1 %section.17 = (bf16[128,4096]{1,0:T(8,128)(2,1)}, bf16[2,2,128,4096]{3,2,1,0:T(8,128)(2,1)}, bf16[2,2,128,512]{3,2,1,0:T(8,128)(2,1)}, bf16[2,128,4096]{2,1,0:T(8,128)(2,1)}) custom-call(s32[2]{0:T(128)} %pad_add_fusion.place_ref, bf16[128,4096]{1,0:T(8,128)(2,1)} %copy-done.24, ...), custom_call_target="tpu_custom_call", output_to_operand_aliasing={{1}: (9, {}), {2}: (10, {}), {3}: (11, {})} | custom-call | tf_op jit(solution)/shard_map/section/pallas_call | solution.py:484
  364.0 1.0 copy-done.7
  365.4 2.5 copy-done.1
  367.9 2.2 copy-done.3
  370.1 5.7 %partial.3 = (bf16[1,2,2,512,128]{4,3,2,1,0:T(8,128)(2,1)}, bf16[6,2,2,512,128]{4,3,2,1,0:T(8,128)(2,1)}) custom-call(s32[14]{0:T(128)S(1)} %stack.333.place_ref, bf16[2,2,128,4096]{3,2,1,0:T(8,128)(2,1)S(1)} %copy-done.3, bf16[2,2,128,4096]{3,2,1,0:T(8,128)(2,1)S(1)} %bitcast.109, f32[2,2,128,128]{3,2,1,0:T(8,128)S(1)} %copy-done.10, ...), custom_call_target="tpu_custom_call" | custom-call | tf_op jit(solution)/shard_map/partial/pallas_call | solution.py:515
  375.8 7.6 %collective-permute-start.27 = (bf16[6,2,2,512,128]{4,3,2,1,0:T(8,128)(2,1)}, bf16[6,2,2,512,128]{4,3,2,1,0:T(8,128)(2,1)S(1)}, u32[]{:S(2)}, u32[]{:S(2)}) collective-permute-start(bf16[6,2,2,512,128]{4,3,2,1,0:T(8,128)(2,1)} %get-tuple-element.105), channel_id=1, source_target_pairs={{0,1},{1,0},{2,3},{3,2},{4,5},{5,4},{6,7},{7,6},{8,9},{9,8},{10,11... | collective-permute-start | bytes 9437192 | tf_op jit(solution)/shard_map/ppermute | solution.py:283
  383.6 2.2 copy-done.2
  385.8 2.2 copy-done.4
  388.0 1.2 copy-done.12
  389.2 5.4 %partial.2 = (bf16[7,2,2,512,128]{4,3,2,1,0:T(8,128)(2,1)S(1)}, bf16[2,2,2,512,128]{4,3,2,1,0:T(8,128)(2,1)S(1)}) custom-call(s32[18]{0:T(128)S(1)} %stack.324.place_ref, bf16[2,2,128,4096]{3,2,1,0:T(8,128)(2,1)S(1)} %copy-done.4, bf16[2,2,128,4096]{3,2,1,0:T(8,128)(2,1)S(1)} %bitcast.110, f32[2,2,128,128]{3,2,1,0:T(8,128)S(1)} %copy-done.10, ...), custom_call_target="tpu_custom_call" | custom-call | tf_op jit(solution)/shard_map/partial/pallas_call | solution.py:515
  394.7 2.3 plus.9
  397.8 7.8 %collective-permute-done.29 = bf16[2,2,512,128]{3,2,1,0:T(8,128)(2,1)} collective-permute-done((bf16[2,2,512,128]{3,2,1,0:T(8,128)(2,1)}, bf16[2,2,512,128]{3,2,1,0:T(8,128)(2,1)}, u32[]{:S(2)}, u32[]{:S(2)}) %collective-permute-start.29) | collective-permute-done | bytes 524320 | tf_op jit(solution)/shard_map/ppermute | solution.py:291
  405.6 1.1 select_bitcast_fusion.1
  406.8 2.0 copy-done.6
  409.0 1.8 collective-permute-start.34
  411.7 5.8 %collective-permute-done.34 = bf16[2,2,512,128]{3,2,1,0:T(8,128)(2,1)S(1)} collective-permute-done((bf16[2,2,512,128]{3,2,1,0:T(8,128)(2,1)S(1)}, bf16[2,2,512,128]{3,2,1,0:T(8,128)(2,1)S(1)}, u32[]{:S(2)}, u32[]{:S(2)}) %collective-permute-start.34) | collective-permute-done | bytes 524320 | tf_op jit(solution)/shard_map/ppermute | solution.py:291
  417.7 2.7 collective-permute-start.35
  420.4 2.7 collective-permute-done.30
  423.3 2.7 collective-permute-start.31
  426.0 2.7 collective-permute-done.35
  428.9 2.7 collective-permute-start.36
  431.6 2.7 collective-permute-done.31
  434.5 2.7 collective-permute-start.32
  437.2 2.7 collective-permute-done.36
  440.1 4.6 %collective-permute-start.37 = (bf16[2,512,128]{2,1,0:T(8,128)(2,1)S(1)}, bf16[2,512,128]{2,1,0:T(8,128)(2,1)S(1)}, u32[]{:S(2)}, u32[]{:S(2)}) collective-permute-start(bf16[2,512,128]{2,1,0:T(8,128)(2,1)S(1)} %slice_bitcast_fusion), channel_id=1, source_target_pairs={{0,1},{1,0},{2,3},{3,2},{4,5},{5,4},{6,7},{7,6},{8,9},{9,8},{10,11... | collective-permute-start | bytes 786440 | tf_op jit(solution)/shard_map/ppermute | solution.py:283
  445.7 4.6 %collective-permute-start.33 = (bf16[2,512,128]{2,1,0:T(8,128)(2,1)S(1)}, bf16[2,512,128]{2,1,0:T(8,128)(2,1)S(1)}, u32[]{:S(2)}, u32[]{:S(2)}) collective-permute-start(bf16[2,512,128]{2,1,0:T(8,128)(2,1)S(1)} %slice_bitcast_fusion.2), channel_id=1, source_target_pairs={{0,1},{1,0},{2,3},{3,2},{4,5},{5,4},{6,7},{7,6},{8,9},{9,8},{10,11... | collective-permute-start | bytes 786440 | tf_op jit(solution)/shard_map/ppermute | solution.py:283
  450.4 2.8 collective-permute-start.38
  453.2 6.7 %collective-permute-done.38 = bf16[2,512,128]{2,1,0:T(8,128)(2,1)S(1)} collective-permute-done((bf16[2,512,128]{2,1,0:T(8,128)(2,1)S(1)}, bf16[2,512,128]{2,1,0:T(8,128)(2,1)S(1)}, u32[]{:S(2)}, u32[]{:S(2)}) %collective-permute-start.38) | collective-permute-done | bytes 262176 | tf_op jit(solution)/shard_map/ppermute | solution.py:287
  (135 shorter events, 29.3 us)
Async XLA Ops:
  0.6 22.1 %copy-start.19 = (s32[2,1,128]{2,1,0:T(1,128)S(1)}, s32[2,1,128]{2,1,0:T(1,128)}, u32[]{:S(2)}) copy-start(s32[2,1,128]{2,1,0:T(1,128)} %seg_row_ref.1) | copy-start | bytes 3076
  0.6 22.3 %copy-start.16 = (bf16[1,2,2,128,512]{4,3,2,1,0:T(8,128)(2,1)S(1)}, bf16[1,2,2,128,512]{4,3,2,1,0:T(8,128)(2,1)}, u32[]{:S(2)}) copy-start(bf16[1,2,2,128,512]{4,3,2,1,0:T(8,128)(2,1)} %param.9) | copy-start | bytes 1572868
  0.7 22.3 %copy-start.17 = (bf16[1,2,2,128,512]{4,3,2,1,0:T(8,128)(2,1)S(1)}, bf16[1,2,2,128,512]{4,3,2,1,0:T(8,128)(2,1)}, u32[]{:S(2)}) copy-start(bf16[1,2,2,128,512]{4,3,2,1,0:T(8,128)(2,1)} %param.10) | copy-start | bytes 1572868
  0.7 4.7 %collective-permute-start = (bf16[2,128,512]{2,1,0:T(8,128)(2,1)}, bf16[2,128,512]{2,1,0:T(8,128)(2,1)S(1)}, u32[]{:S(2)}, u32[]{:S(2)}) collective-permute-start(bf16[2,128,512]{2,1,0:T(8,128)(2,1)} %bitcast.133), channel_id=1, source_target_pairs={{0,1},{1,0},{2,3},{3,2},{4,5},{5,4},{6,7},{7,6},{8,9},{9,8},{10,11... | collective-permute-start | bytes 786440 | tf_op jit(solution)/shard_map/ppermute | solution.py:283
  6.4 21.2 %copy-start.20 = (bf16[2,2,128,512]{3,2,1,0:T(8,128)(2,1)}, bf16[2,2,128,512]{3,2,1,0:T(8,128)(2,1)S(1)}, u32[]{:S(2)}) copy-start(bf16[2,2,128,512]{3,2,1,0:T(8,128)(2,1)S(1)} %pad_maximum_fusion.refs_0_) | copy-start | bytes 1572868
  6.4 10.9 %collective-permute-start.1 = (bf16[2,2,128,512]{3,2,1,0:T(8,128)(2,1)S(1)}, bf16[2,2,128,512]{3,2,1,0:T(8,128)(2,1)S(1)}, u32[]{:S(2)}, u32[]{:S(2)}) collective-permute-start(bf16[2,2,128,512]{3,2,1,0:T(8,128)(2,1)S(1)} %pad_maximum_fusion.refs_0_), channel_id=1, source_target_pairs={{0,4},{1,29},{2,6},{3,31},{4,8},{5,1},{6,10},{7,3},{8,12},{9,5},{1... | collective-permute-start | bytes 1572872 | tf_op jit(solution)/shard_map/ppermute | solution.py:291
  10.3 6.9 %collective-permute-start.2 = (bf16[2,128,512]{2,1,0:T(8,128)(2,1)}, bf16[2,128,512]{2,1,0:T(8,128)(2,1)S(1)}, u32[]{:S(2)}, u32[]{:S(2)}) collective-permute-start(bf16[2,128,512]{2,1,0:T(8,128)(2,1)} %bitcast.134), channel_id=1, source_target_pairs={{0,2},{1,3},{2,0},{3,1},{4,6},{5,7},{6,4},{7,5},{8,10},{9,11},{10,... | collective-permute-start | bytes 786440 | tf_op jit(solution)/shard_map/ppermute | solution.py:287
  17.2 27.5 %copy-start.31 = (bf16[2,2,128,512]{3,2,1,0:T(8,128)(2,1)}, bf16[2,2,128,512]{3,2,1,0:T(8,128)(2,1)S(1)}, u32[]{:S(2)}) copy-start(bf16[2,2,128,512]{3,2,1,0:T(8,128)(2,1)S(1)} %collective-permute-done.1.refs_1_) | copy-start | bytes 1572868
  17.2 2.0 collective-permute-start.8
  19.3 8.3 %copy-start.21 = (bf16[2,2,128,512]{3,2,1,0:T(8,128)(2,1)}, bf16[2,2,128,512]{3,2,1,0:T(8,128)(2,1)S(1)}, u32[]{:S(2)}) copy-start(bf16[2,2,128,512]{3,2,1,0:T(8,128)(2,1)S(1)} %pad_maximum_fusion.1.refs_7_) | copy-start | bytes 1572868
  19.3 10.5 %collective-permute-start.9 = (bf16[2,2,128,512]{3,2,1,0:T(8,128)(2,1)S(1)}, bf16[2,2,128,512]{3,2,1,0:T(8,128)(2,1)S(1)}, u32[]{:S(2)}, u32[]{:S(2)}) collective-permute-start(bf16[2,2,128,512]{3,2,1,0:T(8,128)(2,1)S(1)} %pad_maximum_fusion.1.refs_7_), channel_id=1, source_target_pairs={{0,4},{1,29},{2,6},{3,31},{4,8},{5,1},{6,10},{7,3},{8,12},{9,5},{1... | collective-permute-start | bytes 1572872 | tf_op jit(solution)/shard_map/ppermute | solution.py:291
  22.9 2.2 copy-start
  29.1 8.3 %collective-permute-start.4 = (bf16[2,2,128,512]{3,2,1,0:T(8,128)(2,1)S(1)}, bf16[2,2,128,512]{3,2,1,0:T(8,128)(2,1)}, u32[]{:S(2)}, u32[]{:S(2)}) collective-permute-start(bf16[2,2,128,512]{3,2,1,0:T(8,128)(2,1)S(1)} %collective-permute-done.1.refs_1_), channel_id=1, source_target_pairs={{0,4},{1,29},{2,6},{3,31},{4,8},{5,1},{6,10},{7,3},{8,12},{9,5},{1... | collective-permute-start | bytes 1572872 | tf_op jit(solution)/shard_map/ppermute | solution.py:291
  29.8 36.8 %copy-start.32 = (bf16[2,2,128,512]{3,2,1,0:T(8,128)(2,1)}, bf16[2,2,128,512]{3,2,1,0:T(8,128)(2,1)S(1)}, u32[]{:S(2)}) copy-start(bf16[2,2,128,512]{3,2,1,0:T(8,128)(2,1)S(1)} %collective-permute-done.9.refs_8_) | copy-start | bytes 1572868
  29.9 13.2 %collective-permute-start.11 = (bf16[2,2,128,512]{3,2,1,0:T(8,128)(2,1)S(1)}, bf16[2,2,128,512]{3,2,1,0:T(8,128)(2,1)S(1)}, u32[]{:S(2)}, u32[]{:S(2)}) collective-permute-start(bf16[2,2,128,512]{3,2,1,0:T(8,128)(2,1)S(1)} %collective-permute-done.9.refs_8_), channel_id=1, source_target_pairs={{0,4},{1,29},{2,6},{3,31},{4,8},{5,1},{6,10},{7,3},{8,12},{9,5},{1... | collective-permute-start | bytes 1572872 | tf_op jit(solution)/shard_map/ppermute | solution.py:291
  37.4 11.2 %collective-permute-start.6 = (bf16[2,2,128,512]{3,2,1,0:T(8,128)(2,1)}, bf16[2,2,128,512]{3,2,1,0:T(8,128)(2,1)S(1)}, u32[]{:S(2)}, u32[]{:S(2)}) collective-permute-start(bf16[2,2,128,512]{3,2,1,0:T(8,128)(2,1)} %collective-permute-done.4.refs_3_), channel_id=1, source_target_pairs={{0,4},{1,29},{2,6},{3,31},{4,8},{5,1},{6,10},{7,3},{8,12},{9,5},{1... | collective-permute-start | bytes 1572872 | tf_op jit(solution)/shard_map/ppermute | solution.py:291
  43.1 23.6 %copy-start.33 = (bf16[2,2,128,512]{3,2,1,0:T(8,128)(2,1)}, bf16[2,2,128,512]{3,2,1,0:T(8,128)(2,1)S(1)}, u32[]{:S(2)}) copy-start(bf16[2,2,128,512]{3,2,1,0:T(8,128)(2,1)S(1)} %collective-permute-done.11.refs_10_) | copy-start | bytes 1572868
  43.1 10.9 %collective-permute-start.13 = (bf16[2,2,128,512]{3,2,1,0:T(8,128)(2,1)S(1)}, bf16[2,2,128,512]{3,2,1,0:T(8,128)(2,1)S(1)}, u32[]{:S(2)}, u32[]{:S(2)}) collective-permute-start(bf16[2,2,128,512]{3,2,1,0:T(8,128)(2,1)S(1)} %collective-permute-done.11.refs_10_), channel_id=1, source_target_pairs={{0,4},{1,29},{2,6},{3,31},{4,8},{5,1},{6,10},{7,3},{8,12},{9,5},{1... | collective-permute-start | bytes 1572872 | tf_op jit(solution)/shard_map/ppermute | solution.py:291
  44.7 11.9 %collective-permute-start.3 = (bf16[2,2,128,512]{3,2,1,0:T(8,128)(2,1)S(1)}, bf16[2,2,128,512]{3,2,1,0:T(8,128)(2,1)S(1)}, u32[]{:S(2)}, u32[]{:S(2)}) collective-permute-start(bf16[2,2,128,512]{3,2,1,0:T(8,128)(2,1)S(1)} %collective-permute-done.1.refs_1_), channel_id=1, source_target_pairs={{0,1},{1,0},{2,3},{3,2},{4,5},{5,4},{6,7},{7,6},{8,9},{9,8},{10,11... | collective-permute-start | bytes 1572872 | tf_op jit(solution)/shard_map/ppermute | solution.py:283
  44.7 12.0 %collective-permute-start.5 = (bf16[2,2,128,512]{3,2,1,0:T(8,128)(2,1)}, bf16[2,2,128,512]{3,2,1,0:T(8,128)(2,1)S(1)}, u32[]{:S(2)}, u32[]{:S(2)}) collective-permute-start(bf16[2,2,128,512]{3,2,1,0:T(8,128)(2,1)} %collective-permute-done.4.refs_3_), channel_id=1, source_target_pairs={{0,1},{1,0},{2,3},{3,2},{4,5},{5,4},{6,7},{7,6},{8,9},{9,8},{10,11... | collective-permute-start | bytes 1572872 | tf_op jit(solution)/shard_map/ppermute | solution.py:283
  48.7 18.0 %copy-start.22 = (bf16[2,2,128,512]{3,2,1,0:T(8,128)(2,1)}, bf16[2,2,128,512]{3,2,1,0:T(8,128)(2,1)S(1)}, u32[]{:S(2)}) copy-start(bf16[2,2,128,512]{3,2,1,0:T(8,128)(2,1)S(1)} %collective-permute-done.6.refs_5_) | copy-start | bytes 1572868
  54.0 12.6 %copy-start.23 = (bf16[2,2,128,512]{3,2,1,0:T(8,128)(2,1)}, bf16[2,2,128,512]{3,2,1,0:T(8,128)(2,1)S(1)}, u32[]{:S(2)}) copy-start(bf16[2,2,128,512]{3,2,1,0:T(8,128)(2,1)S(1)} %collective-permute-done.13.refs_12_) | copy-start | bytes 1572868
  54.1 8.5 %collective-permute-start.15 = (bf16[2,2,128,512]{3,2,1,0:T(8,128)(2,1)S(1)}, bf16[2,2,128,512]{3,2,1,0:T(8,128)(2,1)}, u32[]{:S(2)}, u32[]{:S(2)}) collective-permute-start(bf16[2,2,128,512]{3,2,1,0:T(8,128)(2,1)S(1)} %broadcast_select_fusion), channel_id=1, source_target_pairs={{0,4},{1,29},{2,6},{3,31},{4,8},{5,1},{6,10},{7,3},{8,12},{9,5},{1... | collective-permute-start | bytes 1572872 | tf_op jit(solution)/shard_map/ppermute | solution.py:291
  56.1 9.9 %collective-permute-start.10 = (bf16[2,2,128,512]{3,2,1,0:T(8,128)(2,1)S(1)}, bf16[2,2,128,512]{3,2,1,0:T(8,128)(2,1)}, u32[]{:S(2)}, u32[]{:S(2)}) collective-permute-start(bf16[2,2,128,512]{3,2,1,0:T(8,128)(2,1)S(1)} %collective-permute-done.9.refs_8_), channel_id=1, source_target_pairs={{0,1},{1,0},{2,3},{3,2},{4,5},{5,4},{6,7},{7,6},{8,9},{9,8},{10,11... | collective-permute-start | bytes 1572872 | tf_op jit(solution)/shard_map/ppermute | solution.py:283
  56.1 9.9 %collective-permute-start.7 = (bf16[2,2,128,512]{3,2,1,0:T(8,128)(2,1)S(1)}, bf16[2,2,128,512]{3,2,1,0:T(8,128)(2,1)}, u32[]{:S(2)}, u32[]{:S(2)}) collective-permute-start(bf16[2,2,128,512]{3,2,1,0:T(8,128)(2,1)S(1)} %collective-permute-done.6.refs_5_), channel_id=1, source_target_pairs={{0,1},{1,0},{2,3},{3,2},{4,5},{5,4},{6,7},{7,6},{8,9},{9,8},{10,11... | collective-permute-start | bytes 1572872 | tf_op jit(solution)/shard_map/ppermute | solution.py:283
  56.6 10.0 %copy-start.34 = (bf16[2,2,128,512]{3,2,1,0:T(8,128)(2,1)}, bf16[2,2,128,512]{3,2,1,0:T(8,128)(2,1)S(1)}, u32[]{:S(2)}) copy-start(bf16[2,2,128,512]{3,2,1,0:T(8,128)(2,1)S(1)} %collective-permute-done.3.refs_2_) | copy-start | bytes 1572868
  56.6 9.4 %collective-permute-start.12 = (bf16[2,2,128,512]{3,2,1,0:T(8,128)(2,1)S(1)}, bf16[2,2,128,512]{3,2,1,0:T(8,128)(2,1)S(1)}, u32[]{:S(2)}, u32[]{:S(2)}) collective-permute-start(bf16[2,2,128,512]{3,2,1,0:T(8,128)(2,1)S(1)} %collective-permute-done.11.refs_10_), channel_id=1, source_target_pairs={{0,1},{1,0},{2,3},{3,2},{4,5},{5,4},{6,7},{7,6},{8,9},{9,8},{10,11... | collective-permute-start | bytes 1572872 | tf_op jit(solution)/shard_map/ppermute | solution.py:283
  56.7 5.9 %copy-start.35 = (bf16[2,2,128,512]{3,2,1,0:T(8,128)(2,1)}, bf16[2,2,128,512]{3,2,1,0:T(8,128)(2,1)S(1)}, u32[]{:S(2)}) copy-start(bf16[2,2,128,512]{3,2,1,0:T(8,128)(2,1)S(1)} %collective-permute-done.5.refs_4_) | copy-start | bytes 1572868
  56.7 9.3 %collective-permute-start.14 = (bf16[2,2,128,512]{3,2,1,0:T(8,128)(2,1)S(1)}, bf16[2,2,128,512]{3,2,1,0:T(8,128)(2,1)}, u32[]{:S(2)}, u32[]{:S(2)}) collective-permute-start(bf16[2,2,128,512]{3,2,1,0:T(8,128)(2,1)S(1)} %collective-permute-done.13.refs_12_), channel_id=1, source_target_pairs={{0,1},{1,0},{2,3},{3,2},{4,5},{5,4},{6,7},{7,6},{8,9},{9,8},{10,11... | collective-permute-start | bytes 1572872 | tf_op jit(solution)/shard_map/ppermute | solution.py:283
  62.6 4.0 collective-permute-start.16
  80.0 4.0 collective-permute-start.19
  82.0 2.0 collective-permute-start.17
  82.7 1.3 collective-permute-start.18
  86.3 1.4 collective-permute-start.20
  90.1 1.4 collective-permute-start.21
  93.5 1.4 collective-permute-start.22
  96.9 1.4 collective-permute-start.23
  100.4 1.4 collective-permute-start.24
  103.8 216.1 %collective-permute-start.25 = (bf16[128,4096]{1,0:T(8,128)(2,1)}, bf16[128,4096]{1,0:T(8,128)(2,1)S(1)}, u32[]{:S(2)}, u32[]{:S(2)}) collective-permute-start(bf16[128,4096]{1,0:T(8,128)(2,1)} %get-tuple-element.92), channel_id=1, source_target_pairs={{32,0},{64,32},{33,1},{65,33},{34,2},{66,34},{35,3},{67,35},{36,4}... | collective-permute-start | bytes 3145736 | tf_op jit(solution)/shard_map/ppermute | solution.py:494
  331.6 20.2 %collective-permute-start.26 = (bf16[128,4096]{1,0:T(8,128)(2,1)}, bf16[128,4096]{1,0:T(8,128)(2,1)S(1)}, u32[]{:S(2)}, u32[]{:S(2)}) collective-permute-start(bf16[128,4096]{1,0:T(8,128)(2,1)} %get-tuple-element.96), channel_id=1, source_target_pairs={{32,0},{33,1},{34,2},{35,3},{36,4},{37,5},{38,6},{39,7},{40,8},{41... | collective-permute-start | bytes 3145736 | tf_op jit(solution)/shard_map/ppermute | solution.py:494
  352.8 11.1 %copy-start.18 = (bf16[2,2,128,512]{3,2,1,0:T(8,128)(2,1)S(1)}, bf16[2,2,128,512]{3,2,1,0:T(8,128)(2,1)}, u32[]{:S(2)}) copy-start(bf16[2,2,128,512]{3,2,1,0:T(8,128)(2,1)} %get-tuple-element.102.mixed_ref) | copy-start | bytes 1572868
  352.8 12.5 %copy-start.10 = (f32[2,2,128,128]{3,2,1,0:T(8,128)S(1)}, f32[2,2,128,128]{3,2,1,0:T(8,128)}, u32[]{:S(2)}) copy-start(f32[2,2,128,128]{3,2,1,0:T(8,128)} %copy-done.9) | copy-start | bytes 786436
  352.9 12.5 %copy-start.13 = (f32[1,2,4096]{2,1,0:T(2,128)S(1)}, f32[1,2,4096]{2,1,0:T(2,128)}, u32[]{:S(2)}) copy-start(f32[1,2,4096]{2,1,0:T(2,128)} %param.13) | copy-start | bytes 98308
  365.3 10.5 %copy-start.11 = (bf16[2,512,512]{2,1,0:T(8,128)(2,1)}, bf16[2,512,512]{2,1,0:T(8,128)(2,1)S(1)}, u32[]{:S(2)}) copy-start(bf16[2,512,512]{2,1,0:T(8,128)(2,1)S(1)} %factors.1.right_ref) | copy-start | bytes 3145732
  365.4 2.6 copy-start.1
  367.9 2.2 copy-start.3
  375.8 30.9 %collective-permute-start.27 = (bf16[6,2,2,512,128]{4,3,2,1,0:T(8,128)(2,1)}, bf16[6,2,2,512,128]{4,3,2,1,0:T(8,128)(2,1)S(1)}, u32[]{:S(2)}, u32[]{:S(2)}) collective-permute-start(bf16[6,2,2,512,128]{4,3,2,1,0:T(8,128)(2,1)} %get-tuple-element.105), channel_id=1, source_target_pairs={{0,1},{1,0},{2,3},{3,2},{4,5},{5,4},{6,7},{7,6},{8,9},{9,8},{10,11... | collective-permute-start | bytes 9437192 | tf_op jit(solution)/shard_map/ppermute | solution.py:283
  383.4 11.2 %collective-permute-start.28 = (bf16[1,2,2,512,128]{4,3,2,1,0:T(8,128)(2,1)}, bf16[1,2,2,512,128]{4,3,2,1,0:T(8,128)(2,1)}, u32[]{:S(2)}, u32[]{:S(2)}) collective-permute-start(bf16[1,2,2,512,128]{4,3,2,1,0:T(8,128)(2,1)} %get-tuple-element.106), channel_id=1, source_target_pairs={{0,1},{1,0},{2,3},{3,2},{4,5},{5,4},{6,7},{7,6},{8,9},{9,8},{10,11... | collective-permute-start | bytes 1572872 | tf_op jit(solution)/shard_map/ppermute | solution.py:283
  383.6 2.2 copy-start.2
  385.8 2.2 copy-start.4
  394.6 2.3 copy-start.5
  394.6 2.3 copy-start.14
  397.0 8.7 %collective-permute-start.29 = (bf16[2,2,512,128]{3,2,1,0:T(8,128)(2,1)}, bf16[2,2,512,128]{3,2,1,0:T(8,128)(2,1)}, u32[]{:S(2)}, u32[]{:S(2)}) collective-permute-start(bf16[2,2,512,128]{3,2,1,0:T(8,128)(2,1)} %plus.9), channel_id=1, source_target_pairs={{0,4},{1,29},{2,6},{3,31},{4,8},{5,1},{6,10},{7,3},{8,12},{9,5},{1... | collective-permute-start | bytes 1572872 | tf_op jit(solution)/shard_map/ppermute | solution.py:291
  406.8 2.0 copy-start.6
  409.0 8.4 %collective-permute-start.34 = (bf16[2,2,512,128]{3,2,1,0:T(8,128)(2,1)S(1)}, bf16[2,2,512,128]{3,2,1,0:T(8,128)(2,1)S(1)}, u32[]{:S(2)}, u32[]{:S(2)}) collective-permute-start(bf16[2,2,512,128]{3,2,1,0:T(8,128)(2,1)S(1)} %plus.14), channel_id=1, source_target_pairs={{0,4},{1,29},{2,6},{3,31},{4,8},{5,1},{6,10},{7,3},{8,12},{9,5},{1... | collective-permute-start | bytes 1572872 | tf_op jit(solution)/shard_map/ppermute | solution.py:291
  411.1 12.0 %collective-permute-start.30 = (bf16[2,2,512,128]{3,2,1,0:T(8,128)(2,1)S(1)}, bf16[2,2,512,128]{3,2,1,0:T(8,128)(2,1)S(1)}, u32[]{:S(2)}, u32[]{:S(2)}) collective-permute-start(bf16[2,2,512,128]{3,2,1,0:T(8,128)(2,1)S(1)} %plus.10), channel_id=1, source_target_pairs={{0,4},{1,29},{2,6},{3,31},{4,8},{5,1},{6,10},{7,3},{8,12},{9,5},{1... | collective-permute-start | bytes 1572872 | tf_op jit(solution)/shard_map/ppermute | solution.py:291
  417.7 11.0 %collective-permute-start.35 = (bf16[2,2,512,128]{3,2,1,0:T(8,128)(2,1)S(1)}, bf16[2,2,512,128]{3,2,1,0:T(8,128)(2,1)S(1)}, u32[]{:S(2)}, u32[]{:S(2)}) collective-permute-start(bf16[2,2,512,128]{3,2,1,0:T(8,128)(2,1)S(1)} %plus.15), channel_id=1, source_target_pairs={{0,4},{1,29},{2,6},{3,31},{4,8},{5,1},{6,10},{7,3},{8,12},{9,5},{1... | collective-permute-start | bytes 1572872 | tf_op jit(solution)/shard_map/ppermute | solution.py:291
  423.3 11.0 %collective-permute-start.31 = (bf16[2,2,512,128]{3,2,1,0:T(8,128)(2,1)S(1)}, bf16[2,2,512,128]{3,2,1,0:T(8,128)(2,1)S(1)}, u32[]{:S(2)}, u32[]{:S(2)}) collective-permute-start(bf16[2,2,512,128]{3,2,1,0:T(8,128)(2,1)S(1)} %plus.11), channel_id=1, source_target_pairs={{0,4},{1,29},{2,6},{3,31},{4,8},{5,1},{6,10},{7,3},{8,12},{9,5},{1... | collective-permute-start | bytes 1572872 | tf_op jit(solution)/shard_map/ppermute | solution.py:291
  428.9 11.0 %collective-permute-start.36 = (bf16[2,2,512,128]{3,2,1,0:T(8,128)(2,1)S(1)}, bf16[2,2,512,128]{3,2,1,0:T(8,128)(2,1)S(1)}, u32[]{:S(2)}, u32[]{:S(2)}) collective-permute-start(bf16[2,2,512,128]{3,2,1,0:T(8,128)(2,1)S(1)} %plus.16), channel_id=1, source_target_pairs={{0,4},{1,29},{2,6},{3,31},{4,8},{5,1},{6,10},{7,3},{8,12},{9,5},{1... | collective-permute-start | bytes 1572872 | tf_op jit(solution)/shard_map/ppermute | solution.py:291
  434.3 5.6 %copy-start.15 = (bf16[2,2,2,512,128]{4,3,2,1,0:T(8,128)(2,1)S(1)}, bf16[2,2,2,512,128]{4,3,2,1,0:T(8,128)(2,1)}, u32[]{:S(2)}) copy-start(bf16[2,2,2,512,128]{4,3,2,1,0:T(8,128)(2,1)} %copy-done.14) | copy-start | bytes 3145732
  434.5 11.0 %collective-permute-start.32 = (bf16[2,2,512,128]{3,2,1,0:T(8,128)(2,1)S(1)}, bf16[2,2,512,128]{3,2,1,0:T(8,128)(2,1)S(1)}, u32[]{:S(2)}, u32[]{:S(2)}) collective-permute-start(bf16[2,2,512,128]{3,2,1,0:T(8,128)(2,1)S(1)} %plus.12), channel_id=1, source_target_pairs={{0,4},{1,29},{2,6},{3,31},{4,8},{5,1},{6,10},{7,3},{8,12},{9,5},{1... | collective-permute-start | bytes 1572872 | tf_op jit(solution)/shard_map/ppermute | solution.py:291
  440.1 10.2 %collective-permute-start.37 = (bf16[2,512,128]{2,1,0:T(8,128)(2,1)S(1)}, bf16[2,512,128]{2,1,0:T(8,128)(2,1)S(1)}, u32[]{:S(2)}, u32[]{:S(2)}) collective-permute-start(bf16[2,512,128]{2,1,0:T(8,128)(2,1)S(1)} %slice_bitcast_fusion), channel_id=1, source_target_pairs={{0,1},{1,0},{2,3},{3,2},{4,5},{5,4},{6,7},{7,6},{8,9},{9,8},{10,11... | collective-permute-start | bytes 786440 | tf_op jit(solution)/shard_map/ppermute | solution.py:283
  445.7 7.5 %collective-permute-start.33 = (bf16[2,512,128]{2,1,0:T(8,128)(2,1)S(1)}, bf16[2,512,128]{2,1,0:T(8,128)(2,1)S(1)}, u32[]{:S(2)}, u32[]{:S(2)}) collective-permute-start(bf16[2,512,128]{2,1,0:T(8,128)(2,1)S(1)} %slice_bitcast_fusion.2), channel_id=1, source_target_pairs={{0,1},{1,0},{2,3},{3,2},{4,5},{5,4},{6,7},{7,6},{8,9},{9,8},{10,11... | collective-permute-start | bytes 786440 | tf_op jit(solution)/shard_map/ppermute | solution.py:283
  450.4 9.5 %collective-permute-start.38 = (bf16[2,512,128]{2,1,0:T(8,128)(2,1)S(1)}, bf16[2,512,128]{2,1,0:T(8,128)(2,1)S(1)}, u32[]{:S(2)}, u32[]{:S(2)}) collective-permute-start(bf16[2,512,128]{2,1,0:T(8,128)(2,1)S(1)} %fusion), channel_id=1, source_target_pairs={{0,2},{1,3},{2,0},{3,1},{4,6},{5,7},{6,4},{7,5},{8,10},{9,11},{10,... | collective-permute-start | bytes 786440 | tf_op jit(solution)/shard_map/ppermute | solution.py:287
  (12 other events, 11.5 us)
